TPU v7x, 512 devices: a whole 4x4x16 slice. The times are simulated.
512 devices in a mesh: train: 64 (over z_lo, y, core), tensor: 8 (over z_hi, x).
Axes of the slice: x: 4, y: 4, z: 16 (z_hi: 2, z_lo: 8; z = z_hi * 8 + z_lo), core: 2. Of those that a mesh axis runs over, the one named last changes fastest.
Arguments:
- core_left: float32 [32, 65536], P('tensor', 'train'), may hold values from -0.5 to 0.5
- core_right: float32 [16, 196608], P('tensor', 'train'), may hold values from -0.5 to 0.5
- grad_left: float32 [32, 65536], P('tensor', 'train'), may hold values from -6 to 6
- grad_right: float32 [16, 196608], P('tensor', 'train'), may hold values from -6 to 6
- first_left: float32 [32, 65536], P('tensor', 'train'), may hold values from -0.625 to 0.625
- first_right: float32 [16, 196608], P('tensor', 'train'), may hold values from -0.625 to 0.625
- second_left: float32 [32, 65536], P('tensor', 'train'), may hold values from 0.05 to 1
- second_right: float32 [16, 196608], P('tensor', 'train'), may hold values from 0.05 to 1
- up_base: bfloat16 [64, 1536, 4096], P('train', 'tensor'), may hold values from -0.09375 to 0.09375
- down_base: bfloat16 [64, 1536, 4096], P('train', 'tensor'), may hold values from -0.15625 to 0.15625
- states: bfloat16 [4, 512, 4096], P(None, 'train'), may hold values from -6 to 6
- routes: int32 [4, 512, 8], P(None, 'train'), may hold values from 0 to 63, all different within a row; in each aligned block of 8 rows (0 to 7, 8 to 15, ..., all dimensions but the last counted through in order) at most 2 rows name the same one
- gates: float32 [4, 512, 8], P(None, 'train'), may hold values from 0.1 to 0.4
Outputs:
- mixed: bfloat16 [4, 512, 4096], P(None, 'train', 'tensor')
- left_next: float32 [32, 65536], P('tensor', 'train')
- right_next: float32 [16, 196608], P('tensor', 'train')
- first_left_next: float32 [32, 65536], P('tensor', 'train')
- first_right_next: float32 [16, 196608], P('tensor', 'train')
- second_left_next: float32 [32, 65536], P('tensor', 'train')
- second_right_next: float32 [16, 196608], P('tensor', 'train')
Inputs may be any that keep to these rules, and one draw needn't show every extreme that they name: `routes`: each row names 8 different experts; among the 8 rows n with n // 8 equal, for one step, no expert is named more than 2 times.
All inputs are finite; a program needn't handle non-finite values.
Results may differ from a plain program's by a relative error of at most 0.019.
Values may be sent and summed in bfloat16 or wider, within the bound.
A program may use at most 64 MiB of HBM per device.

v0:
```python
import jax
import jax.numpy as jnp
from jax import lax
from jax.sharding import PartitionSpec as P

I1 = 64
RANK = 16
I2 = 64
J2 = 48


BETA_ONE = 0.9
BETA_TWO = 0.999
LEARN_RATE = 0.01
WEIGHT_DECAY = 0.1
EPSILON = 1e-08
STEP_NUMBER = 10.0


def adamw_update(value_now, gradient, first_moment, second_moment):
    first_next = BETA_ONE * first_moment + (1.0 - BETA_ONE) * gradient
    second_next = BETA_TWO * second_moment + (1.0 - BETA_TWO) * gradient * gradient
    first_scale = 1.0 - BETA_ONE**STEP_NUMBER
    second_scale = 1.0 - BETA_TWO**STEP_NUMBER
    update = first_next / first_scale / (jnp.sqrt(second_next / second_scale) + EPSILON)
    value_next = value_now - LEARN_RATE * (update + WEIGHT_DECAY * value_now)
    return (value_next, first_next, second_next)


def body(
    core_left,
    core_right,
    grad_left,
    grad_right,
    first_left,
    first_right,
    second_left,
    second_right,
    up_base,
    down_base,
    states,
    routes,
    gates,
):
    left_next, first_left_next, second_left_next = adamw_update(
        core_left, grad_left, first_left, second_left
    )
    right_next, first_right_next, second_right_next = adamw_update(
        core_right, grad_right, first_right, second_right
    )
    experts = lax.axis_size("train")
    left_split = left_next.astype(jnp.bfloat16).reshape(left_next.shape[0], -1, experts)
    right_split = right_next.astype(jnp.bfloat16).reshape(right_next.shape[0], -1, experts)
    left_all, right_all = (
        lax.all_gather(left_split, "train", axis=1, tiled=True),
        lax.all_gather(right_split, "train", axis=1, tiled=True),
    )
    own_index = lax.axis_index("train")
    left_own = lax.dynamic_slice_in_dim(left_all, own_index, 1, 2)[:, :, 0]
    right_own = lax.dynamic_slice_in_dim(right_all, own_index, 1, 2)[:, :, 0]
    right_full = lax.all_gather(right_own, "tensor", axis=0, tiled=True)
    left_three = left_own.reshape(left_own.shape[0], I1, RANK)
    right_three = right_full.reshape(RANK, J2, I2)
    width = states.shape[2]
    delta = jnp.einsum(
        "jar,rkb->jkab", left_three, right_three, preferred_element_type=jnp.float32
    ).reshape(left_own.shape[0] * J2, width)
    up_eff = (up_base[0].astype(jnp.float32) + delta).astype(jnp.bfloat16)
    down_local = down_base[0]
    rows_dev = states.shape[1]
    top_count = routes.shape[2]
    capacity = max(2, 2 * rows_dev * top_count // experts)
    slot_count = experts * capacity
    outputs = []
    for step_index in range(states.shape[0]):
        rows_here = states[step_index]
        expert_ids = routes[step_index].reshape(-1)
        weights = gates[step_index]
        onehot = (expert_ids[:, None] == jnp.arange(experts, dtype=jnp.int32)[None, :]).astype(
            jnp.int32
        )
        before = jnp.cumsum(onehot, axis=0) - onehot
        slot_index = jnp.sum(before * onehot, axis=1)
        target = expert_ids * capacity + slot_index
        slot_onehot = (target[:, None] == jnp.arange(slot_count, dtype=jnp.int32)[None, :]).astype(
            jnp.float32
        )
        per_row = slot_onehot.reshape(rows_dev, top_count, slot_count)
        dispatch_matrix = jnp.sum(per_row, axis=1).T.astype(jnp.bfloat16)
        combine_matrix = jnp.sum(per_row * weights[:, :, None], axis=1)
        buffer = jnp.dot(dispatch_matrix, rows_here, preferred_element_type=jnp.float32).astype(
            jnp.bfloat16
        )
        buffer = buffer.reshape(experts, capacity, rows_here.shape[1])
        hidden = jax.nn.silu(
            jnp.einsum(
                "scd,fd->scf",
                lax.all_to_all(buffer, "train", split_axis=0, concat_axis=0, tiled=True),
                up_eff,
                preferred_element_type=jnp.float32,
            )
        ).astype(jnp.bfloat16)
        partial_out = jnp.einsum(
            "scf,fd->scd", hidden, down_local, preferred_element_type=jnp.float32
        )
        summed = lax.psum_scatter(
            partial_out.astype(jnp.bfloat16), "tensor", scatter_dimension=2, tiled=True
        ).astype(jnp.float32)
        returned = lax.all_to_all(
            summed.astype(jnp.bfloat16), "train", split_axis=0, concat_axis=0, tiled=True
        ).astype(summed.dtype)
        flat_back = returned.reshape(slot_count, -1)
        mixed_rows = jnp.dot(combine_matrix, flat_back, precision=lax.Precision.HIGHEST)
        outputs.append(mixed_rows.astype(jnp.bfloat16))
    mixed = jnp.stack(outputs, axis=0)
    return (
        mixed,
        left_next,
        right_next,
        first_left_next,
        first_right_next,
        second_left_next,
        second_right_next,
    )


def solution(mesh):
    in_specs = (
        P("tensor", "train"),
        P("tensor", "train"),
        P("tensor", "train"),
        P("tensor", "train"),
        P("tensor", "train"),
        P("tensor", "train"),
        P("tensor", "train"),
        P("tensor", "train"),
        P("train", "tensor", None),
        P("train", "tensor", None),
        P(None, "train", None),
        P(None, "train", None),
        P(None, "train", None),
    )
    out_specs = (
        P(None, "train", "tensor"),
        P("tensor", "train"),
        P("tensor", "train"),
        P("tensor", "train"),
        P("tensor", "train"),
        P("tensor", "train"),
        P("tensor", "train"),
    )
    return jax.shard_map(body, mesh=mesh, in_specs=in_specs, out_specs=out_specs, check_vma=False)
```

profile of v0, /device:TPU:6, one launch (start us, length us, event | category | flops | bytes accessed | tf_op | source)
XLA Modules:
  0.0 965.3 jit_solution(17156549139410537262)
XLA Ops:
  14.6 16.3 %all-to-all-start.6 = ((bf16[64,2,4096]{2,1,0:T(2,128)(2,1)}), bf16[64,2,4096]{2,1,0:T(2,128)(2,1)S(1)}, u32[]{:S(2)}, u32[]{:S(2)}) async-start(bf16[64,2,4096]{2,1,0:T(2,128)(2,1)} %reshape.150), calls=%async_computation.9 | async-start | bytes 2097152 | tf_op jit(solution)/shard_map/all_to_all | solution.py:98
  32.4 2.5 reshape.148
  34.9 47.3 %all-to-all-done.6 = bf16[64,2,4096]{2,1,0:T(2,128)(2,1)S(1)} async-done(((bf16[64,2,4096]{2,1,0:T(2,128)(2,1)}), bf16[64,2,4096]{2,1,0:T(2,128)(2,1)S(1)}, u32[]{:S(2)}, u32[]{:S(2)}) %all-to-all-start.6) | async-done | bytes 1048608 | tf_op jit(solution)/shard_map/all_to_all | solution.py:98
  82.3 8.2 all-to-all-start.4
  91.3 134.0 %all_gather.9 = bf16[2,3072,64]{2,0,1:T(2,128)(2,1)S(1)} all-gather(bf16[2,48,64]{2,0,1:T(2,128)(2,1)S(1)} %copy.65), channel_id=1, replica_groups=mesh['train'=64,'tensor'=8] {'train'}, dimensions={1}, use_global_device_ids=true | all-gather | bytes 798720 | tf_op jit(solution)/shard_map/all_gather | solution.py:56
  225.3 1.9 constant_dynamic-slice_fusion.1
  228.8 63.2 %all-gather = bf16[16,3072,1]{1,2,0:T(2,128)(2,1)S(1)} all-gather(bf16[2,3072,1]{1,2,0:T(2,128)(2,1)S(1)} %copy.66), channel_id=2, replica_groups=mesh['train'=64,'tensor'=8] {'tensor'}, dimensions={0}, use_global_device_ids=true | all-gather | bytes 110592 | tf_op jit(solution)/shard_map/all_gather | solution.py:61
  294.9 5.7 all-to-all-start.2
  301.4 132.4 %all_gather.11 = bf16[4,1024,64]{2,0,1:T(4,128)(2,1)S(1)} all-gather(bf16[4,16,64]{2,0,1:T(4,128)(2,1)S(1)} %copy.67), channel_id=1, replica_groups=mesh['train'=64,'tensor'=8] {'train'}, dimensions={1}, use_global_device_ids=true | all-gather | bytes 532480 | tf_op jit(solution)/shard_map/all_gather | solution.py:55
  435.2 3.7 convolution_bitcast_fusion
  438.9 6.6 copy.71
  445.5 5.9 reshape.144
  451.4 2.7 fusion.1
  454.1 4.0 convolution_convert_fusion
  459.7 2.5 reshape.140
  462.2 5.5 all-to-all-start
  467.8 4.0 convolution_convert_fusion.2
  471.8 4.0 convolution_convert_fusion.4
  476.2 61.9 %all-to-all-done = bf16[64,2,4096]{2,1,0:T(2,128)(2,1)} async-done(((bf16[64,2,4096]{2,1,0:T(2,128)(2,1)}), bf16[64,2,4096]{2,1,0:T(2,128)(2,1)}, u32[]{:S(2)}, u32[]{:S(2)}) %all-to-all-start) | async-done | bytes 1048608 | tf_op jit(solution)/shard_map/all_to_all | solution.py:98
  538.1 4.0 convolution_convert_fusion.6
  542.1 52.2 %reduce-scatter.11.cloned.1.call-done = bf16[64,2,512]{2,0,1:T(8,128)(2,1)} async-done(((bf16[64,2,4096]{2,0,1:T(8,128)(2,1)}), bf16[64,2,512]{2,0,1:T(8,128)(2,1)}) %reduce-scatter.11.cloned.1.call-update) | async-done | bytes 131088 | tf_op jit(solution)/shard_map/reduce_scatter | solution.py:106
  594.3 1.7 copy.79
  596.0 5.6 all-to-all-start.7
  601.6 106.8 %reduce-scatter.9.cloned.1.call-done = bf16[64,2,512]{2,0,1:T(8,128)(2,1)} async-done(((bf16[64,2,4096]{2,0,1:T(8,128)(2,1)}), bf16[64,2,512]{2,0,1:T(8,128)(2,1)}) %reduce-scatter.9.cloned.1.call-update) | async-done | bytes 131088 | tf_op jit(solution)/shard_map/reduce_scatter | solution.py:106
  710.1 5.6 all-to-all-start.5
  715.7 106.5 %reduce-scatter.7.cloned.1.call-done = bf16[64,2,512]{2,0,1:T(8,128)(2,1)} async-done(((bf16[64,2,4096]{2,0,1:T(8,128)(2,1)}), bf16[64,2,512]{2,0,1:T(8,128)(2,1)}) %reduce-scatter.7.cloned.1.call-update) | async-done | bytes 131088 | tf_op jit(solution)/shard_map/reduce_scatter | solution.py:106
  822.2 1.7 copy.75
  823.9 5.6 all-to-all-start.3
  829.6 106.5 %reduce-scatter.5.cloned.1.call-done = bf16[64,2,512]{2,0,1:T(8,128)(2,1)} async-done(((bf16[64,2,4096]{2,0,1:T(8,128)(2,1)}), bf16[64,2,512]{2,0,1:T(8,128)(2,1)}) %reduce-scatter.5.cloned.1.call-update) | async-done | bytes 131088 | tf_op jit(solution)/shard_map/reduce_scatter | solution.py:106
  936.1 1.7 copy.73
  937.8 5.6 all-to-all-start.1
  944.1 13.9 %all-to-all-done.1 = bf16[64,2,512]{2,1,0:T(2,128)(2,1)S(1)} async-done(((bf16[64,2,512]{2,1,0:T(2,128)(2,1)}), bf16[64,2,512]{2,1,0:T(2,128)(2,1)S(1)}, u32[]{:S(2)}, u32[]{:S(2)}) %all-to-all-start.1) | async-done | bytes 131104 | tf_op jit(solution)/shard_map/all_to_all | solution.py:109
  (88 shorter events, 21.3 us)
Async XLA Ops:
  7.2 447.0 %copy-start = (bf16[1,192,4096]{2,1,0:T(8,128)(2,1)S(1)}, bf16[1,192,4096]{2,1,0:T(8,128)(2,1)}, u32[]{:S(2)}) copy-start(bf16[1,192,4096]{2,1,0:T(8,128)(2,1)} %param.22) | copy-start | bytes 4718596
  14.6 16.3 %copy-start.2 = (bf16[4,8,4096]{2,1,0:T(8,128)(2,1)S(1)}, bf16[4,8,4096]{2,1,0:T(8,128)(2,1)}, u32[]{:S(2)}) copy-start(bf16[4,8,4096]{2,1,0:T(8,128)(2,1)} %param.23) | copy-start | bytes 786436
  14.6 67.7 %all-to-all-start.6 = ((bf16[64,2,4096]{2,1,0:T(2,128)(2,1)}), bf16[64,2,4096]{2,1,0:T(2,128)(2,1)S(1)}, u32[]{:S(2)}, u32[]{:S(2)}) async-start(bf16[64,2,4096]{2,1,0:T(2,128)(2,1)} %reshape.150), calls=%async_computation.9 | async-start | bytes 2097152 | tf_op jit(solution)/shard_map/all_to_all | solution.py:98
  34.9 55.5 %copy-start.3 = (f32[2,3072]{1,0:T(2,128)S(1)}, f32[2,3072]{1,0:T(2,128)}, u32[]{:S(2)}) copy-start(f32[2,3072]{1,0:T(2,128)} %param.14) | copy-start | bytes 73732
  34.9 55.6 %copy-start.4 = (f32[2,3072]{1,0:T(2,128)S(1)}, f32[2,3072]{1,0:T(2,128)}, u32[]{:S(2)}) copy-start(f32[2,3072]{1,0:T(2,128)} %param.16) | copy-start | bytes 73732
  34.9 55.6 %copy-start.5 = (f32[2,3072]{1,0:T(2,128)S(1)}, f32[2,3072]{1,0:T(2,128)}, u32[]{:S(2)}) copy-start(f32[2,3072]{1,0:T(2,128)} %param.18) | copy-start | bytes 73732
  34.9 55.6 %copy-start.6 = (f32[2,3072]{1,0:T(2,128)S(1)}, f32[2,3072]{1,0:T(2,128)}, u32[]{:S(2)}) copy-start(f32[2,3072]{1,0:T(2,128)} %param.20) | copy-start | bytes 73732
  82.3 9.1 copy-start.1
  82.3 212.6 %all-to-all-start.4 = ((bf16[64,2,4096]{2,1,0:T(2,128)(2,1)}), bf16[64,2,4096]{2,1,0:T(2,128)(2,1)}, u32[]{:S(2)}, u32[]{:S(2)}) async-start(bf16[64,2,4096]{2,1,0:T(2,128)(2,1)} %reshape.148), calls=%async_computation.6 | async-start | bytes 2097152 | tf_op jit(solution)/shard_map/all_to_all | solution.py:98
  294.9 5.7 copy-start.7
  294.9 5.7 copy-start.8
  294.9 5.8 copy-start.9
  294.9 5.8 copy-start.10
  294.9 167.3 %all-to-all-start.2 = ((bf16[64,2,4096]{2,1,0:T(2,128)(2,1)}), bf16[64,2,4096]{2,1,0:T(2,128)(2,1)}, u32[]{:S(2)}, u32[]{:S(2)}) async-start(bf16[64,2,4096]{2,1,0:T(2,128)(2,1)} %reshape.146), calls=%async_computation.3 | async-start | bytes 2097152 | tf_op jit(solution)/shard_map/all_to_all | solution.py:98
  300.5 293.7 %reduce-scatter.11.cloned.1.call-start = ((), (), s32[]{:S(2)}) async-start(), calls=%async_computation.15 | async-start | bytes 1179648 | tf_op jit(solution)/shard_map/reduce_scatter | solution.py:106
  462.2 75.9 %all-to-all-start = ((bf16[64,2,4096]{2,1,0:T(2,128)(2,1)}), bf16[64,2,4096]{2,1,0:T(2,128)(2,1)}, u32[]{:S(2)}, u32[]{:S(2)}) async-start(bf16[64,2,4096]{2,1,0:T(2,128)(2,1)} %reshape.140), calls=%async_computation | async-start | bytes 2097152 | tf_op jit(solution)/shard_map/all_to_all | solution.py:98
  467.7 240.7 %reduce-scatter.9.cloned.1.call-start = ((), (), s32[]{:S(2)}) async-start(), calls=%async_computation.14 | async-start | bytes 1179648 | tf_op jit(solution)/shard_map/reduce_scatter | solution.py:106
  471.8 350.4 %reduce-scatter.7.cloned.1.call-start = ((), (), s32[]{:S(2)}) async-start(), calls=%async_computation.13 | async-start | bytes 1179648 | tf_op jit(solution)/shard_map/reduce_scatter | solution.py:106
  475.9 460.2 %reduce-scatter.5.cloned.1.call-start = ((), (), s32[]{:S(2)}) async-start(), calls=%async_computation.12 | async-start | bytes 1179648 | tf_op jit(solution)/shard_map/reduce_scatter | solution.py:106
  596.0 114.1 %all-to-all-start.7 = ((bf16[64,2,512]{2,1,0:T(2,128)(2,1)}), bf16[64,2,512]{2,1,0:T(2,128)(2,1)S(1)}, u32[]{:S(2)}, u32[]{:S(2)}) async-start(bf16[64,2,512]{2,1,0:T(2,128)(2,1)} %copy.79), calls=%async_computation.11 | async-start | bytes 262144 | tf_op jit(solution)/shard_map/all_to_all | solution.py:109
  710.1 113.8 %all-to-all-start.5 = ((bf16[64,2,512]{2,1,0:T(2,128)(2,1)}), bf16[64,2,512]{2,1,0:T(2,128)(2,1)S(1)}, u32[]{:S(2)}, u32[]{:S(2)}) async-start(bf16[64,2,512]{2,1,0:T(2,128)(2,1)} %copy.77), calls=%async_computation.8 | async-start | bytes 262144 | tf_op jit(solution)/shard_map/all_to_all | solution.py:109
  823.9 113.9 %all-to-all-start.3 = ((bf16[64,2,512]{2,1,0:T(2,128)(2,1)}), bf16[64,2,512]{2,1,0:T(2,128)(2,1)S(1)}, u32[]{:S(2)}, u32[]{:S(2)}) async-start(bf16[64,2,512]{2,1,0:T(2,128)(2,1)} %copy.75), calls=%async_computation.5 | async-start | bytes 262144 | tf_op jit(solution)/shard_map/all_to_all | solution.py:109
  937.8 20.2 %all-to-all-start.1 = ((bf16[64,2,512]{2,1,0:T(2,128)(2,1)}), bf16[64,2,512]{2,1,0:T(2,128)(2,1)S(1)}, u32[]{:S(2)}, u32[]{:S(2)}) async-start(bf16[64,2,512]{2,1,0:T(2,128)(2,1)} %copy.73), calls=%async_computation.2 | async-start | bytes 262144 | tf_op jit(solution)/shard_map/all_to_all | solution.py:109
Sparse Core Ops, SparseCore 0:
  458.3 135.9 reduce-scatter.10
  599.5 108.8 reduce-scatter.8
  712.9 109.2 reduce-scatter.6
  827.3 108.7 reduce-scatter.4
where the time goes:
time: 968 us; the launch traced here: 965 us
  waiting for transfers between devices  495 us (51%)
  blocking collectives  330 us (34%)
  starting transfers between devices  58.5 us (6%)
  local copies, waits for them, and re-layouts  35.1 us (4%)
  matrix products  25.1 us (3%)
  between operations  14.1 us (1%)
    reduce_scatter x4, waiting for transfers between devices, body(): lax.psum_scatter(partial_out.astype(jnp.bfloat16), 'tensor', scatter_dime...  372 us
    all_gather x1, blocking collectives, body(): lax.all_gather(right_split, 'train', axis=1, tiled=True)  134 us
    all_gather x1, blocking collectives, body(): lax.all_gather(left_split, 'train', axis=1, tiled=True)  132 us
    all_to_all x4, waiting for transfers between devices, body(): lax.all_to_all(buffer, 'train', split_axis=0, concat_axis=0, tiled=True)  109 us
    all_gather x1, blocking collectives, body(): right_full = lax.all_gather(right_own, 'tensor', axis=0, tiled=True)  63.2 us
    all_to_all x4, starting transfers between devices, body(): lax.all_to_all(buffer, 'train', split_axis=0, concat_axis=0, tiled=True)  35.6 us
    all_to_all x4, starting transfers between devices, body(): lax.all_to_all(summed.astype(jnp.bfloat16), 'train', split_axis=0, concat...  22.5 us
  transfers between devices with their start and end apart: 12, of which 7 were waited for; matrix products, arithmetic and copies ran while one was open for 6% of the time, Pallas kernels for 0%

commit v1 on v0

v1 whole, which is shorter than its diff:
```python
import jax
import jax.numpy as jnp
from jax import lax
from jax.experimental import pallas as pl
from jax.experimental.pallas import tpu as pltpu
from jax.sharding import PartitionSpec as P

MESH = pl.DeviceIdType.MESH
BF16 = jnp.bfloat16
F32 = jnp.float32

BETA_ONE = 0.9
BETA_TWO = 0.999
LEARN_RATE = 0.01
WEIGHT_DECAY = 0.1
EPSILON = 1e-08
STEP_NUMBER = 10.0

VMEM_LIMIT = 48 * 1024 * 1024


def adamw_update(value_now, gradient, first_moment, second_moment):
    first_next = BETA_ONE * first_moment + (1.0 - BETA_ONE) * gradient
    second_next = BETA_TWO * second_moment + (1.0 - BETA_TWO) * gradient * gradient
    first_scale = 1.0 - BETA_ONE**STEP_NUMBER
    second_scale = 1.0 - BETA_TWO**STEP_NUMBER
    update = first_next / first_scale / (jnp.sqrt(second_next / second_scale) + EPSILON)
    value_next = value_now - LEARN_RATE * (update + WEIGHT_DECAY * value_now)
    return (value_next, first_next, second_next)


class Place:
    def __init__(self):
        self.train = lax.axis_index("train")
        self.tensor = lax.axis_index("tensor")
        self.core = self.train % 2
        self.y = (self.train // 2) % 4
        self.z_lo = self.train // 8
        self.x = self.tensor % 4
        self.z_hi = self.tensor // 4
        self.z = self.z_hi * 8 + self.z_lo

    def at_z(self, z):
        z = (z + 16) % 16
        return ((z % 8) * 8 + self.y * 2 + self.core, (z // 8) * 4 + self.x)

    def at_y(self, y):
        return (self.z_lo * 8 + ((y + 4) % 4) * 2 + self.core, self.tensor)

    def at_x(self, x):
        return (self.train, self.z_hi * 4 + (x + 4) % 4)

    def twin(self):
        return (self.train + 1 - 2 * self.core, self.tensor)

    def other_half(self):
        return (self.train, (1 - self.z_hi) * 4 + self.x)


def push(src, dst, sems, index, device):
    copy = pltpu.make_async_remote_copy(
        src_ref=src,
        dst_ref=dst,
        send_sem=sems.at[0, index],
        recv_sem=sems.at[1, index],
        device_id=device,
        device_id_type=MESH,
    )
    copy.start()
    return copy


def signal(device):
    pl.semaphore_signal(
        pltpu.get_barrier_semaphore(), inc=1, device_id=device, device_id_type=MESH
    )


def gather_kernel(
    up, down, rows, message,
    up_all, down_all, rows_all, message_all, relay,
    local_sem, z_sem, y_sem, far_sem, twin_sem, weight_sem, relay_sem, small_sem, spread_sem,
):
    at = Place()
    train, tensor, x, y, z_lo, core = at.train, at.tensor, at.x, at.y, at.z_lo, at.core

    @pl.loop(1, 64)
    def _(step):
        signal(((train + step) % 64, tensor))

    for device in (at.at_z(at.z + 1), at.at_z(at.z - 1), at.other_half()):
        signal(device)
    for step in (1, 2, 3):
        signal(at.at_x(x + step))
    pl.semaphore_wait(pltpu.get_barrier_semaphore(), 69)

    weights = ((up, up_all), (down, down_all))
    own = []
    for w, (src, dst) in enumerate(weights):
        for half in (0, 1):
            columns = pl.ds(pl.multiple_of((half * 4 + x) * 512, 512), 512)
            own.append((src.at[:, columns], dst.at[half, x]))
    own.append((rows, rows_all.at[z_lo, y, core]))
    own.append((message.at[train], message_all.at[tensor, train]))
    own = [pltpu.make_async_copy(s, d, local_sem.at[i]) for i, (s, d) in enumerate(own)]
    for copy in own:
        copy.start()

    sent = []
    first = rows_all.at[z_lo, y, core]
    z_right = [push(rows, first, z_sem, 0, at.at_z(at.z + 1))]
    z_left = [push(rows, first, z_sem, 4, at.at_z(at.z - 1))]
    y_right = [push(rows, first, y_sem, 0, at.at_y(y + 1))]
    y_left = [push(rows, first, y_sem, 8, at.at_y(y - 1))]

    def small(step):
        target = (train + step) % 64
        return pltpu.make_async_remote_copy(
            src_ref=message.at[target],
            dst_ref=message_all.at[tensor, train],
            send_sem=small_sem.at[0],
            recv_sem=small_sem.at[1],
            device_id=(target, tensor),
            device_id_type=MESH,
        )

    @pl.loop(1, 64)
    def _(step):
        small(step).start()

    direct, onward = [], {}
    for w, (src, dst) in enumerate(weights):
        for way, step in ((0, 1), (1, -1)):
            far = (x + 2) % 4
            columns = pl.ds(pl.multiple_of((way * 4 + far) * 512, 512), 512)
            direct.append(
                push(src.at[:, columns], relay.at[w, way], relay_sem, w * 2 + way, at.at_x(x + step))
            )
            near = (x + step + 4) % 4
            for half in (0, 1):
                columns = pl.ds(pl.multiple_of((half * 4 + near) * 512, 512), 512)
                sent.append(
                    push(
                        src.at[:, columns], dst.at[half, x],
                        weight_sem, w * 4 + way * 2 + half, at.at_x(near),
                    )
                )

    def pass_on(w):
        dst = weights[w][1]
        for way, step in ((0, 1), (1, -1)):
            direct[w * 2 + way].wait_recv()
            source = (x - step + 4) % 4
            onward[w, way] = push(
                relay.at[w, way], dst.at[way, source],
                relay_sem, 4 + w * 2 + way, at.at_x(x + step),
            )

    blocks = [z_lo]
    for order in range(1, 8):
        step = (order + 1) // 2
        if order % 2 == 1:
            z_right[step - 1].wait_recv()
            block = (z_lo - step + 8) % 8
            if step < 4:
                here = rows_all.at[block, y, core]
                z_right.append(push(here, here, z_sem, step, at.at_z(at.z + 1)))
        else:
            z_left[step - 1].wait_recv()
            block = (z_lo + step) % 8
            if step < 3:
                here = rows_all.at[block, y, core]
                z_left.append(push(here, here, z_sem, 4 + step, at.at_z(at.z - 1)))
        blocks.append(block)
        here = rows_all.at[block, y, core]
        y_right.append(push(here, here, y_sem, order, at.at_y(y + 1)))
        y_left.append(push(here, here, y_sem, 8 + order, at.at_y(y - 1)))

    all_but_one = pltpu.make_async_remote_copy(
        src_ref=message.at[pl.ds(0, 63)],
        dst_ref=message_all.at[tensor, pl.ds(0, 63)],
        send_sem=small_sem.at[0],
        recv_sem=small_sem.at[1],
        device_id=(train, tensor),
        device_id_type=MESH,
    )
    all_but_one.wait_recv()
    own[5].wait()
    here = message_all.at[tensor]
    across = push(here, here, spread_sem, 0, at.other_half())
    spread = [push(here, here, spread_sem, step, at.at_x(x + step)) for step in (1, 2, 3)]

    far_copies = []
    for order, block in enumerate(blocks):
        y_right[order].wait_recv()
        y_left[order].wait_recv()
        if order % 2 == 0:
            here = rows_all.at[block, (y + 3) % 4, core]
            far_copies.append(push(here, here, far_sem, order, at.at_y(y + 1)))
        else:
            here = rows_all.at[block, (y + 1) % 4, core]
            far_copies.append(push(here, here, far_sem, order, at.at_y(y - 1)))

    pass_on(0)

    across.wait_recv()
    here = message_all.at[(1 - at.z_hi) * 4 + x]
    for step in (1, 2, 3):
        spread.append(push(here, here, spread_sem, 3 + step, at.at_x(x + step)))

    own[4].wait()
    twin_copies = []
    for order, block in enumerate(blocks):
        far_copies[order].wait_recv()
        here = rows_all.at[block, :, core]
        twin_copies.append(push(here, here, twin_sem, order, at.twin()))

    pass_on(1)

    for copy in spread + sent + list(onward.values()) + twin_copies:
        copy.wait_recv()
    for copy in own[:4]:
        copy.wait()
    for copy in (
        z_right + z_left + y_right + y_left + far_copies + twin_copies
        + [across] + spread + sent + direct + list(onward.values()) + [all_but_one]
    ):
        copy.wait_send()


def dma_sems(count):
    return pltpu.SemaphoreType.DMA((2, count))


def gather_all(up, down, rows, message):
    return pl.pallas_call(
        gather_kernel,
        out_shape=(
            jax.ShapeDtypeStruct((2, 4, 192, 512), BF16),
            jax.ShapeDtypeStruct((2, 4, 192, 512), BF16),
            jax.ShapeDtypeStruct((8, 4, 2, 32, 1024), BF16),
            jax.ShapeDtypeStruct((8, 64, 2, 128), F32),
            jax.ShapeDtypeStruct((2, 2, 192, 512), BF16),
        ),
        in_specs=[pl.BlockSpec(memory_space=pl.ANY)] * 4,
        out_specs=[pl.BlockSpec(memory_space=pl.ANY)] * 5,
        scratch_shapes=[
            pltpu.SemaphoreType.DMA((6,)),
            dma_sems(7),
            dma_sems(16),
            dma_sems(8),
            dma_sems(8),
            dma_sems(8),
            dma_sems(8),
            pltpu.SemaphoreType.DMA((2,)),
            dma_sems(7),
        ],
        compiler_params=pltpu.CompilerParams(collective_id=0, has_side_effects=True),
        name="gather_all",
    )(up, down, rows, message)


def up_kernel(up_ref, left_ref, right_ref, rows_ref, out_ref, weight, total):
    half = pl.program_id(1)
    for j in range(4):
        for lane in range(4):
            lanes = slice(lane * 128, lane * 128 + 128)
            delta = jnp.zeros((48, 128), F32)
            for r in range(16):
                delta = delta + right_ref[r] * left_ref[j, r : r + 1, lanes]
            units = slice(j * 48, j * 48 + 48)
            weight[units, lanes] = (up_ref[units, lanes].astype(F32) + delta).astype(BF16)
    term = lax.dot_general(
        weight[...], rows_ref[...], (((1,), (1,)), ((), ())), preferred_element_type=F32
    )

    @pl.when(half == 0)
    def _():
        total[...] = term

    @pl.when(half == 1)
    def _():
        out_ref[...] = (total[...] + term).astype(BF16)


def up_project(up_all, left, right, rows):
    return pl.pallas_call(
        up_kernel,
        grid=(4, 2),
        out_shape=jax.ShapeDtypeStruct((4, 192, 512), BF16),
        in_specs=[
            pl.BlockSpec((None, None, 192, 512), lambda g, h: (h, g, 0, 0)),
            pl.BlockSpec((None, None, 4, 16, 512), lambda g, h: (h, g, 0, 0, 0)),
            pl.BlockSpec((16, 48, 128), lambda g, h: (0, 0, 0)),
            pl.BlockSpec((512, 512), lambda g, h: (0, h)),
        ],
        out_specs=pl.BlockSpec((None, 192, 512), lambda g, h: (g, 0, 0)),
        scratch_shapes=[pltpu.VMEM((192, 512), BF16), pltpu.VMEM((192, 512), F32)],
        compiler_params=pltpu.CompilerParams(vmem_limit_bytes=VMEM_LIMIT),
        name="up_project",
    )(up_all, left, right, rows)


def hidden_kernel(part, out, far, near, passed, hidden, far_sem, near_sem, out_sem):
    at = Place()
    x = at.x
    right, left = at.at_x(x + 1), at.at_x(x - 1)
    signal(right)
    signal(left)
    pl.semaphore_wait(pltpu.get_barrier_semaphore(), 2)

    right_x, left_x, far_x = (x + 1) % 4, (x + 3) % 4, (x + 2) % 4
    top, low = pl.ds(0, 96), pl.ds(96, 96)
    copies = [
        push(part.at[far_x, top], far.at[0], far_sem, 0, right),
        push(part.at[far_x, low], far.at[1], far_sem, 1, left),
        push(part.at[right_x, low], near.at[0, low], near_sem, 0, right),
        push(part.at[left_x, top], near.at[1, top], near_sem, 1, left),
    ]
    copies[0].wait_recv()
    passed[0] = (part[right_x, top].astype(F32) + far[0].astype(F32)).astype(BF16)
    copies.append(push(passed.at[0], near.at[0, top], near_sem, 2, right))
    copies[1].wait_recv()
    passed[1] = (part[left_x, low].astype(F32) + far[1].astype(F32)).astype(BF16)
    copies.append(push(passed.at[1], near.at[1, low], near_sem, 3, left))
    for copy in copies[2:]:
        copy.wait_recv()

    value = part[x].astype(F32) + near[0].astype(F32) + near[1].astype(F32)
    hidden[x] = (value / (1.0 + jnp.exp(-value))).astype(BF16)
    here = hidden.at[x]
    from_left = push(here, here, out_sem, 0, right)
    from_right = push(here, here, out_sem, 1, left)
    from_left.wait_recv()
    here = hidden.at[left_x, top]
    far_top = push(here, here, out_sem, 2, right)
    from_right.wait_recv()
    here = hidden.at[right_x, low]
    far_low = push(here, here, out_sem, 3, left)
    far_top.wait_recv()
    far_low.wait_recv()
    for copy in copies + [from_left, from_right, far_top, far_low]:
        copy.wait_send()
    out[...] = hidden[...]


def hidden_sum(part):
    return pl.pallas_call(
        hidden_kernel,
        out_shape=jax.ShapeDtypeStruct((4, 192, 512), BF16),
        in_specs=[pl.BlockSpec(memory_space=pltpu.VMEM)],
        out_specs=pl.BlockSpec(memory_space=pltpu.VMEM),
        scratch_shapes=[
            pltpu.VMEM((2, 96, 512), BF16),
            pltpu.VMEM((2, 192, 512), BF16),
            pltpu.VMEM((2, 96, 512), BF16),
            pltpu.VMEM((4, 192, 512), BF16),
            dma_sems(2),
            dma_sems(4),
            dma_sems(4),
        ],
        compiler_params=pltpu.CompilerParams(
            collective_id=1, has_side_effects=True, vmem_limit_bytes=VMEM_LIMIT
        ),
        name="hidden_sum",
    )(part)


def down_kernel(hidden_ref, down_ref, combine_ref, out_ref):
    part = lax.dot_general(
        hidden_ref[...], down_ref[...], (((0,), (0,)), ((), ())), preferred_element_type=F32
    ).astype(BF16)
    for group in range(8):
        mixed = jnp.dot(
            combine_ref[group], part[group * 64 : group * 64 + 64], preferred_element_type=F32
        ).astype(BF16)
        for y in range(4):
            for core in range(2):
                at = (y * 2 + core) * 32
                out_ref[core, y, group] = mixed[at : at + 32]


def down_project(hidden, down_all, combine):
    return pl.pallas_call(
        down_kernel,
        grid=(2,),
        out_shape=jax.ShapeDtypeStruct((2, 4, 16, 32, 512), BF16),
        in_specs=[
            pl.BlockSpec((768, 512), lambda h: (0, 0)),
            pl.BlockSpec((None, 768, 512), lambda h: (h, 0, 0)),
            pl.BlockSpec((8, 256, 64), lambda h: (0, 0, 0)),
        ],
        out_specs=pl.BlockSpec((2, 4, 8, 32, 512), lambda h: (0, 0, h, 0, 0)),
        compiler_params=pltpu.CompilerParams(vmem_limit_bytes=VMEM_LIMIT),
        name="down_project",
    )(hidden, down_all, combine)


def add_pairs(dst, count, *terms):
    @pl.loop(0, count)
    def _(i):
        total = terms[0](i).astype(F32)
        for term in terms[1:]:
            total = total + term(i).astype(F32)
        dst[i] = total.astype(BF16)


def mix_kernel(
    part, out, twin_in, sums, far, near, line, right_in, left_in, right_out, left_out,
    twin_sem, far_sem, near_sem, right_sem, left_sem,
):
    at = Place()
    y, z, core = at.y, at.z, at.core
    y_right, y_left = at.at_y(y + 1), at.at_y(y - 1)
    z_right, z_left = at.at_z(z + 1), at.at_z(z - 1)
    for device in (at.twin(), y_right, y_left, z_right, z_left):
        signal(device)
    pl.semaphore_wait(pltpu.get_barrier_semaphore(), 5)

    order = [(y + 2) % 4, (y + 1) % 4, (y + 3) % 4, y]
    twins = [
        push(part.at[1 - core, to], twin_in.at[to], twin_sem, i, at.twin())
        for i, to in enumerate(order)
    ]

    def sum_cores(i):
        to = order[i]
        twins[i].wait_recv()
        add_pairs(sums.at[i], 16, lambda k: part[core, to, k], lambda k: twin_in[to, k])

    top, low = pl.ds(0, 8), pl.ds(8, 8)
    sum_cores(0)
    copies = [
        push(sums.at[0, top], far.at[0], far_sem, 0, y_right),
        push(sums.at[0, low], far.at[1], far_sem, 1, y_left),
    ]
    sum_cores(1)
    copies.append(push(sums.at[1, low], near.at[0, low], near_sem, 0, y_right))
    sum_cores(2)
    copies.append(push(sums.at[2, top], near.at[1, top], near_sem, 1, y_left))
    copies[0].wait_recv()
    add_pairs(sums.at[1], 8, lambda k: sums[1, k], lambda k: far[0, k])
    copies.append(push(sums.at[1, top], near.at[0, top], near_sem, 2, y_right))
    copies[1].wait_recv()
    add_pairs(sums.at[2, low], 8, lambda k: sums[2, 8 + k], lambda k: far[1, k])
    copies.append(push(sums.at[2, low], near.at[1, low], near_sem, 3, y_left))
    sum_cores(3)
    for copy in copies[2:]:
        copy.wait_recv()
    add_pairs(line, 16, lambda k: sums[3, k], lambda k: near[0, k], lambda k: near[1, k])

    rights, lefts = [], []
    for step in range(8):
        value = line[(z + 8 - step) % 16].astype(F32)
        if step > 0:
            rights[step - 1].wait_recv()
            value = value + right_in[step - 1].astype(F32)
        right_out[step] = value.astype(BF16)
        rights.append(push(right_out.at[step], right_in.at[step], right_sem, step, z_right))
        if step < 7:
            value = line[(z + 9 + step) % 16].astype(F32)
            if step > 0:
                lefts[step - 1].wait_recv()
                value = value + left_in[step - 1].astype(F32)
            left_out[step] = value.astype(BF16)
            lefts.append(push(left_out.at[step], left_in.at[step], left_sem, step, z_left))
    lefts[6].wait_recv()
    rights[7].wait_recv()
    value = line[z].astype(F32) + right_in[7].astype(F32) + left_in[6].astype(F32)
    out[...] = value.astype(BF16)
    for copy in twins + copies + rights + lefts:
        copy.wait_send()


def mix_sum(part):
    return pl.pallas_call(
        mix_kernel,
        out_shape=jax.ShapeDtypeStruct((32, 512), BF16),
        in_specs=[pl.BlockSpec(memory_space=pltpu.VMEM)],
        out_specs=pl.BlockSpec(memory_space=pltpu.VMEM),
        scratch_shapes=[
            pltpu.VMEM((4, 16, 32, 512), BF16),
            pltpu.VMEM((4, 16, 32, 512), BF16),
            pltpu.VMEM((2, 8, 32, 512), BF16),
            pltpu.VMEM((2, 16, 32, 512), BF16),
            pltpu.VMEM((16, 32, 512), BF16),
            pltpu.VMEM((8, 32, 512), BF16),
            pltpu.VMEM((7, 32, 512), BF16),
            pltpu.VMEM((8, 32, 512), BF16),
            pltpu.VMEM((7, 32, 512), BF16),
            dma_sems(4),
            dma_sems(2),
            dma_sems(4),
            dma_sems(8),
            dma_sems(7),
        ],
        compiler_params=pltpu.CompilerParams(
            collective_id=2, has_side_effects=True, vmem_limit_bytes=VMEM_LIMIT
        ),
        name="mix_sum",
    )(part)


def body(
    core_left,
    core_right,
    grad_left,
    grad_right,
    first_left,
    first_right,
    second_left,
    second_right,
    up_base,
    down_base,
    states,
    routes,
    gates,
):
    left_next, first_left_next, second_left_next = adamw_update(
        core_left, grad_left, first_left, second_left
    )
    right_next, first_right_next, second_right_next = adamw_update(
        core_right, grad_right, first_right, second_right
    )
    tensor = lax.axis_index("tensor")
    x, z_hi = tensor % 4, tensor // 4

    chosen = (routes[..., None] == jnp.arange(64, dtype=jnp.int32)).astype(F32)
    taken = jnp.sum(chosen, axis=2)
    weight = jnp.sum(chosen * gates[..., None], axis=2)
    earlier = jnp.cumsum(taken, axis=1) - taken
    slot = taken * (earlier + 1.0)
    message = jnp.concatenate(
        [
            lax.reduce_precision(left_next, 8, 7).reshape(64, 64),
            lax.reduce_precision(right_next, 8, 7).reshape(96, 64),
            slot.reshape(32, 64),
            weight.reshape(32, 64),
            jnp.zeros((32, 64), F32),
        ],
        axis=0,
    )
    message = message.T.reshape(64, 2, 128)
    rows = lax.dynamic_index_in_dim(states.reshape(32, 2, 4, 512), x, 2, keepdims=False)
    up_all, down_all, rows_all, message_all, _ = gather_all(
        up_base[0], down_base[0], rows.reshape(32, 1024), message
    )

    message_all = message_all.reshape(8, 64, 256)
    left = lax.dynamic_slice_in_dim(message_all[:, :, :64], z_hi * 4, 4, 0)
    left = left.reshape(4, 2, 4, 8, 4, 16)
    left = lax.dynamic_index_in_dim(left, x, 2, keepdims=False)
    left = left.transpose(1, 0, 3, 4, 2).reshape(512, 8).astype(BF16)
    spread = (jnp.arange(8)[:, None] == jnp.arange(512)[None, :] // 64).astype(BF16)
    left = jnp.dot(left, spread, preferred_element_type=F32).reshape(2, 4, 4, 16, 512)
    right = message_all[:, :, 64:160].reshape(8, 64, 2, 48)
    right = right.transpose(0, 2, 1, 3).reshape(16, 48, 64)
    right = jnp.concatenate([right, right], axis=2)

    own = lax.dynamic_index_in_dim(message_all, tensor, 0, keepdims=False)
    slot = own[:, 160:192].reshape(8, 256)
    weight = own[:, 192:224].reshape(8, 256)
    slots, places = jnp.arange(64), jnp.arange(256)
    match = (slots[:, None] // 2 == places[None, :] // 8)[None] & (
        slot[:, None, :] == (slots % 2 + 1).astype(F32)[None, :, None]
    )
    picked = jnp.einsum(
        "gsr,grd->gsd",
        match.astype(BF16),
        rows_all.reshape(8, 256, 1024),
        preferred_element_type=F32,
    ).astype(BF16)
    match = (slots[None, :] // 2 == places[:, None] // 8)[None] & (
        slot[:, :, None] == (slots % 2 + 1).astype(F32)[None, None, :]
    )
    combine = jnp.where(match, weight[:, :, None], 0.0).astype(BF16)

    part = up_project(up_all, left, right, picked.reshape(512, 1024))
    hidden = hidden_sum(part)
    part = down_project(hidden.reshape(768, 512), down_all.reshape(2, 768, 512), combine)
    mixed = mix_sum(part).reshape(4, 8, 512)
    return (
        mixed,
        left_next,
        right_next,
        first_left_next,
        first_right_next,
        second_left_next,
        second_right_next,
    )


def solution(mesh):
    cores = (P("tensor", "train"),) * 6
    in_specs = cores + (P("tensor", "train"),) * 2 + (
        P("train", "tensor", None),
        P("train", "tensor", None),
        P(None, "train", None),
        P(None, "train", None),
        P(None, "train", None),
    )
    out_specs = (P(None, "train", "tensor"),) + cores
    return jax.shard_map(body, mesh=mesh, in_specs=in_specs, out_specs=out_specs, check_vma=False)
```

time: 968 us -> 168 us (0.17)
  waiting for transfers between devices: 495 us -> 0 us
  blocking collectives: 330 us -> 0 us
  Pallas kernels: 0 us -> 144 us
  starting transfers between devices: 58.5 us -> 0 us
  local copies, waits for them, and re-layouts: 35.1 us -> 11.8 us
  matrix products: 25.1 us -> 3.42 us
  between operations: 14.1 us -> 0.88 us
    reduce_scatter x4 -> x0, waiting for transfers between devices: 372 us -> none  [body(): lax.psum_scatter(partial_out.astype(jnp.bfloat16), 'tensor', scatter_dime...]
    all_gather x3 -> x0, blocking collectives: 330 us -> none  [the longest x1 134 us: body(): lax.all_gather(right_split, 'train', axis=1, tiled=True)]
    pallas_call x0 -> x5, Pallas kernels: none -> 144 us  [the longest x1 64.1 us: gather_all(): pl.pallas_call(gather_kernel, out_shape=(jax.ShapeDtypeStruct((2, 4, 192,...]
    all_to_all x8 -> x0, waiting for transfers between devices: 123 us -> none  [the longest x4 109 us: body(): lax.all_to_all(buffer, 'train', split_axis=0, concat_axis=0, tiled=True)]
    all_to_all x8 -> x0, starting transfers between devices: 58.1 us -> none  [the longest x4 35.6 us: body(): lax.all_to_all(buffer, 'train', split_axis=0, concat_axis=0, tiled=True)]
    dot_general x13 -> x2, matrix products: 25.1 us -> 3.42 us  [the longest x1 3.08 us: body(): jnp.einsum('gsr,grd->gsd', match.astype(BF16), rows_all.reshape(8, 256, 1...]
    reshape x14 -> x7, local copies, waits for them, and re-layouts: 14.6 us -> 4.78 us  [the longest x1 1.46 us: body(): message_all = message_all.reshape(8, 64, 256)]
  transfers between devices with their start and end apart: 12 -> 0, of which waited for: 7 -> 0; matrix products, arithmetic and copies ran while one was open for 6% -> 0% of each run, Pallas kernels for 0% -> 0%
where the time goes in v1:
time: 168 us; the launch traced here: 166 us
  Pallas kernels  144 us (86%)
  local copies, waits for them, and re-layouts  11.8 us (7%)
  other arithmetic  6.3 us (4%)
  matrix products  3.42 us (2%)
    pallas_call x1, Pallas kernels, gather_all(): pl.pallas_call(gather_kernel, out_shape=(jax.ShapeDtypeStruct((2, 4, 192,...  64.1 us
    pallas_call x1, Pallas kernels, mix_sum(): pl.pallas_call(mix_kernel, out_shape=jax.ShapeDtypeStruct((32, 512), BF16...  46.8 us
    pallas_call x1, Pallas kernels, hidden_sum(): pl.pallas_call(hidden_kernel, out_shape=jax.ShapeDtypeStruct((4, 192, 512...  23.6 us
    pallas_call x1, Pallas kernels, up_project(): pl.pallas_call(up_kernel, grid=(4, 2), out_shape=jax.ShapeDtypeStruct((4,...  5.71 us
    unnamed x14, local copies, waits for them, and re-layouts  4.58 us
    pallas_call x1, Pallas kernels, down_project(): pl.pallas_call(down_kernel, grid=(2,), out_shape=jax.ShapeDtypeStruct((2,...  3.67 us

profile of v1, /device:TPU:6, one launch (start us, length us, event | category | flops | bytes accessed | tf_op | source)
XLA Modules:
  0.0 166.4 jit_solution(17432850807888956359)
XLA Ops:
  0.7 0.1 broadcast_compare_fusion.1
  0.8 0.7 broadcast_compare_fusion
  1.5 0.9 select_reduce_fusion
  2.4 1.4 fusion.23
  3.9 0.1 reshape.335
  3.9 1.5 fusion.21
  5.4 0.1 reshape.336
  5.6 0.7 copy.34.message
  6.3 1.1 reshape.333
  7.4 0.4 dynamic-slice_reduce_fusion
  7.9 0.6 copy.38
  8.5 64.1 %gather_all.1 = (bf16[2,4,192,512]{3,2,1,0:T(8,128)(2,1)}, bf16[2,4,192,512]{3,2,1,0:T(8,128)(2,1)}, bf16[8,4,2,32,1024]{4,3,2,1,0:T(8,128)(2,1)}, f32[8,64,2,128]{3,2,1,0:T(2,128)}, bf16[2,2,192,512]{3,2,1,0:T(8,128)(2,1)}) custom-call(bf16[192,4096]{1,0:T(8,128)(2,1)} %bitcast.47, bf16[192,4096]{1,0:T(8,128)(2,1)} %bitcast.48, bf16[32,1024]{1,0:T(8,128)(2,1)} %bitcast.50, ...), custom_call_target="tpu_custom_call" | custom-call | tf_op jit(solution)/shard_map/gather_all/pallas_call | solution.py:236
  72.6 1.5 reshape.339
  74.1 0.1 slice.19
  74.2 0.1 eq.102
  74.3 3.1 %convolution_convert_fusion = bf16[8,64,1024]{2,1,0:T(8,128)(2,1)S(1)} fusion(bf16[8,256,1024]{2,1,0:T(8,128)(2,1)} %bitcast.46, f32[8,256]{1,0:T(8,128)S(1)} %eq.102, f32[64]{0:T(128)S(1)} %get-tuple-element.26, pred[64,256]{1,0:T(8,128)(4,1)S(1)} %broadcast_compare_fusion.1), kind=kOutput, calls=%fused_computation | convolution fusion | flops 269221888 | bytes 5267712 | tf_op jit(solution)/shard_map/gsr,grd->gsd/dot_general | solution.py:567
  77.4 0.1 broadcast_in_dim.13
  77.5 0.8 slice.17
  78.4 0.6 constant_dynamic-slice_fusion.1
  79.0 1.1 copy.37
  80.1 0.2 copy.32
  80.3 0.3 reshape.342
  80.6 0.2 pad_maximum_fusion.right_ref
  80.8 1.0 reshape.340
  81.9 1.5 select_convert_fusion.combine_ref
  83.3 0.3 fusion.6.left_ref
  83.7 5.7 %up_project.1.part = bf16[4,192,512]{2,1,0:T(8,128)(2,1)S(1)} custom-call(bf16[2,4,192,512]{3,2,1,0:T(8,128)(2,1)S(1)} %copy-done.2, f32[2,4,4,16,512]{4,3,2,1,0:T(8,128)S(1)} %fusion.6.left_ref, f32[16,48,128]{2,1,0:T(8,128)S(1)} %pad_maximum_fusion.right_ref, bf16[512,1024]{1,0:T(8,128)(2,1)S(1)} %bitcast.42), custom_call_target="tpu_custom_call" | custom-call | tf_op jit(solution)/shard_map/up_project/pallas_call | solution.py:287
  89.4 23.6 %hidden_sum.1 = bf16[4,192,512]{2,1,0:T(8,128)(2,1)S(1)} custom-call(bf16[4,192,512]{2,1,0:T(8,128)(2,1)S(1)} %up_project.1.part), custom_call_target="tpu_custom_call" | custom-call | tf_op jit(solution)/shard_map/hidden_sum/pallas_call | solution.py:348
  113.1 3.7 %down_project.1.part = bf16[2,4,16,32,512]{4,3,2,1,0:T(8,128)(2,1)} custom-call(bf16[768,512]{1,0:T(8,128)(2,1)S(1)} %bitcast.43, bf16[2,768,512]{2,1,0:T(8,128)(2,1)S(1)} %bitcast.44, bf16[8,256,64]{2,1,0:T(8,128)(2,1)S(1)} %select_convert_fusion.combine_ref), custom_call_target="tpu_custom_call" | custom-call | tf_op jit(solution)/shard_map/down_project/pallas_call | solution.py:384
  116.7 2.2 %copy-done = bf16[2,4,16,32,512]{4,3,2,1,0:T(8,128)(2,1)S(1)} copy-done((bf16[2,4,16,32,512]{4,3,2,1,0:T(8,128)(2,1)S(1)}, bf16[2,4,16,32,512]{4,3,2,1,0:T(8,128)(2,1)}, u32[]{:S(2)}) %copy-start) | copy-done | bytes 4194328
  118.9 46.8 %mix_sum.1 = bf16[32,512]{1,0:T(8,128)(2,1)S(1)} custom-call(bf16[2,4,16,32,512]{4,3,2,1,0:T(8,128)(2,1)S(1)} %copy-done), custom_call_target="tpu_custom_call" | custom-call | tf_op jit(solution)/shard_map/mix_sum/pallas_call | solution.py:476
  165.8 0.6 copy.48
  (20 shorter events, 0.2 us)
Async XLA Ops:
  0.7 73.6 %copy-start.3 = (f32[64]{0:T(128)}, f32[64]{0:T(128)S(1)}, u32[]{:S(2)}) copy-start(f32[64]{0:T(128)S(1)} %get-tuple-element.26) | copy-start | bytes 772
  77.4 6.3 %copy-start.2 = (bf16[2,4,192,512]{3,2,1,0:T(8,128)(2,1)S(1)}, bf16[2,4,192,512]{3,2,1,0:T(8,128)(2,1)}, u32[]{:S(2)}) copy-start(bf16[2,4,192,512]{3,2,1,0:T(8,128)(2,1)} %get-tuple-element.11.up_ref) | copy-start | bytes 4718596
  81.8 31.2 %copy-start.1 = (bf16[2,4,192,512]{3,2,1,0:T(8,128)(2,1)S(1)}, bf16[2,4,192,512]{3,2,1,0:T(8,128)(2,1)}, u32[]{:S(2)}) copy-start(bf16[2,4,192,512]{3,2,1,0:T(8,128)(2,1)} %get-tuple-element.14) | copy-start | bytes 4718596
  116.7 2.2 %copy-start = (bf16[2,4,16,32,512]{4,3,2,1,0:T(8,128)(2,1)S(1)}, bf16[2,4,16,32,512]{4,3,2,1,0:T(8,128)(2,1)}, u32[]{:S(2)}) copy-start(bf16[2,4,16,32,512]{4,3,2,1,0:T(8,128)(2,1)} %down_project.1.part) | copy-start | bytes 12582916

commit v2 on v0

v2 whole, which is shorter than its diff:
```python
import jax
import jax.numpy as jnp
from jax import lax
from jax.experimental import pallas as pl
from jax.experimental.pallas import tpu as pltpu
from jax.sharding import PartitionSpec as P

MESH = pl.DeviceIdType.MESH
BF16 = jnp.bfloat16
F32 = jnp.float32

BETA_ONE = 0.9
BETA_TWO = 0.999
LEARN_RATE = 0.01
WEIGHT_DECAY = 0.1
EPSILON = 1e-08
STEP_NUMBER = 10.0

VMEM_LIMIT = 48 * 1024 * 1024


def adamw_update(value_now, gradient, first_moment, second_moment):
    first_next = BETA_ONE * first_moment + (1.0 - BETA_ONE) * gradient
    second_next = BETA_TWO * second_moment + (1.0 - BETA_TWO) * gradient * gradient
    first_scale = 1.0 - BETA_ONE**STEP_NUMBER
    second_scale = 1.0 - BETA_TWO**STEP_NUMBER
    update = first_next / first_scale / (jnp.sqrt(second_next / second_scale) + EPSILON)
    value_next = value_now - LEARN_RATE * (update + WEIGHT_DECAY * value_now)
    return (value_next, first_next, second_next)


class Place:
    def __init__(self):
        self.train = lax.axis_index("train")
        self.tensor = lax.axis_index("tensor")
        self.core = self.train % 2
        self.y = (self.train // 2) % 4
        self.z_lo = self.train // 8
        self.x = self.tensor % 4
        self.z_hi = self.tensor // 4
        self.z = self.z_hi * 8 + self.z_lo

    def at_z(self, z):
        z = (z + 16) % 16
        return ((z % 8) * 8 + self.y * 2 + self.core, (z // 8) * 4 + self.x)

    def at_y(self, y):
        return (self.z_lo * 8 + ((y + 4) % 4) * 2 + self.core, self.tensor)

    def at_x(self, x):
        return (self.train, self.z_hi * 4 + (x + 4) % 4)

    def twin(self):
        return (self.train + 1 - 2 * self.core, self.tensor)

    def other_half(self):
        return (self.train, (1 - self.z_hi) * 4 + self.x)


def push(src, dst, sems, index, device):
    copy = pltpu.make_async_remote_copy(
        src_ref=src,
        dst_ref=dst,
        send_sem=sems.at[0, index],
        recv_sem=sems.at[1, index],
        device_id=device,
        device_id_type=MESH,
    )
    copy.start()
    return copy


def signal(device):
    pl.semaphore_signal(
        pltpu.get_barrier_semaphore(), inc=1, device_id=device, device_id_type=MESH
    )


def dma_sems(count):
    return pltpu.SemaphoreType.DMA((2, count))


def iota(shape, dim):
    return lax.broadcasted_iota(jnp.int32, shape, dim)


def one_hot(condition):
    return jnp.where(condition, 1.0, 0.0).astype(BF16)


def contract_first(left, right):
    return lax.dot_general(left, right, (((0,), (0,)), ((), ())), preferred_element_type=F32)


def add_blocks(dst, count, *terms):
    @pl.loop(0, count)
    def _(i):
        total = terms[0](i).astype(F32)
        for term in terms[1:]:
            total = total + term(i).astype(F32)
        dst[i] = total.astype(BF16)


def layer_kernel(
    up, down, rows, message, out,
    up_all, down_all, relay, rows_all, message_z, message_y, message_all,
    pick, combine, order_map, right_rows, right_all, left_all, weight, picked,
    part, hidden_far, hidden_near, hidden_pass, hidden,
    mixed, twin_in, sums, far, near, line, right_in, left_in, right_out, left_out,
    local_sem, z_sem, y_sem, far_sem, twin_sem, weight_sem, relay_sem,
    message_sem, spread_sem, hidden_sem, gather_sem,
    core_sem, mix_far_sem, mix_near_sem, right_sem, left_sem,
):
    at = Place()
    tensor, x, y, z_lo, z, core = at.tensor, at.x, at.y, at.z_lo, at.z, at.core
    twin = at.twin()
    x_right, x_left = at.at_x(x + 1), at.at_x(x - 1)
    y_right, y_left = at.at_y(y + 1), at.at_y(y - 1)
    z_right, z_left = at.at_z(z + 1), at.at_z(z - 1)

    def same_half(step):
        return (((z_lo + step) % 8) * 8 + y * 2 + core, tensor)

    for step in range(1, 8):
        signal(same_half(step))
    for step in (1, 2, 3):
        signal(at.at_x(x + step))
        signal(at.at_y(y + step))
    for device in (twin, z_right, z_left, at.other_half()):
        signal(device)
    pl.semaphore_wait(pltpu.get_barrier_semaphore(), 17)

    unsent = []

    def send(src, dst, sems, index, device):
        copy = push(src, dst, sems, index, device)
        unsent.append(copy)
        return copy

    def move(src, dst, index):
        copy = pltpu.make_async_copy(src, dst, local_sem.at[index])
        copy.start()
        return copy

    here = rows_all.at[z_lo, y, core]
    z_rights = [send(rows, here, z_sem, 0, z_right)]
    z_lefts = [send(rows, here, z_sem, 4, z_left)]

    moved_z = move(message.at[z_lo], message_z.at[z_lo], 0)
    by_z = [
        send(message.at[(z_lo + step) % 8], message_z.at[z_lo], message_sem, step, same_half(step))
        for step in range(1, 8)
    ]
    y_rights = [send(rows, here, y_sem, 0, y_right)]
    y_lefts = [send(rows, here, y_sem, 8, y_left)]
    moved_rows = move(rows, here, 1)

    weights = ((up, up_all), (down, down_all))

    def columns_of(half, to):
        return pl.ds(pl.multiple_of((half * 4 + to) * 512, 512), 512)

    def send_weight(w):
        origin, dst = weights[w]
        first, direct = [], []
        for way, device in ((0, x_right), (1, x_left)):
            first.append(
                send(origin.at[:, columns_of(way, (x + 2) % 4)], relay.at[w, way],
                     relay_sem, w * 2 + way, device)
            )
        for way, device, to in ((0, x_right, (x + 1) % 4), (1, x_left, (x + 3) % 4)):
            for half in (0, 1):
                direct.append(
                    send(origin.at[:, columns_of(half, to)], dst.at[half, x],
                         weight_sem, w * 4 + way * 2 + half, device)
                )
        for half in (0, 1):
            direct.append(move(origin.at[:, columns_of(half, x)], dst.at[half, x], 2 + w * 2 + half))
        return first, direct

    def pass_weight(w, first, direct):
        dst = weights[w][1]
        for way, device, source in ((0, x_right, (x + 3) % 4), (1, x_left, (x + 1) % 4)):
            first[way].wait_recv()
            direct.append(
                send(relay.at[w, way], dst.at[way, source], relay_sem, 4 + w * 2 + way, device)
            )

    def arrive(copies, own=()):
        for copy in copies:
            copy.wait_recv()
        for copy in own:
            copy.wait()

    up_first, up_direct = send_weight(0)

    blocks = [z_lo]
    for order in range(1, 8):
        step = (order + 1) // 2
        if order % 2 == 1:
            z_rights[step - 1].wait_recv()
            block = (z_lo - step + 8) % 8
            here = rows_all.at[block, y, core]
            if step < 4:
                z_rights.append(send(here, here, z_sem, step, z_right))
        else:
            z_lefts[step - 1].wait_recv()
            block = (z_lo + step) % 8
            here = rows_all.at[block, y, core]
            if step < 3:
                z_lefts.append(send(here, here, z_sem, 4 + step, z_left))
        blocks.append(block)
        y_rights.append(send(here, here, y_sem, order, y_right))
        y_lefts.append(send(here, here, y_sem, 8 + order, y_left))
        if order == 3:
            arrive(by_z, [moved_z])
            moved_y = move(message_z.at[:, y], message_y.at[:, y], 6)
            by_y = [
                send(message_z.at[:, (y + step) % 4], message_y.at[:, y],
                     message_sem, 7 + step, at.at_y(y + step))
                for step in (1, 2, 3)
            ]
        if order == 5:
            arrive(by_y, [moved_y])
            moved_core = move(message_y.at[:, :, core], message_all.at[tensor, :, :, core], 7)
            by_core = send(message_y.at[:, :, 1 - core], message_all.at[tensor, :, :, core],
                           message_sem, 0, twin)

    arrive([by_core], [moved_core])
    here = message_all.at[tensor]
    across = send(here, here, spread_sem, 0, at.other_half())
    spread = [send(here, here, spread_sem, step, at.at_x(x + step)) for step in (1, 2, 3)]

    far_copies, twin_copies = [], []

    def pass_rows(order):
        block = blocks[order]
        arrive([y_rights[order], y_lefts[order]])
        if order % 2 == 0:
            here, device = rows_all.at[block, (y + 3) % 4, core], y_right
        else:
            here, device = rows_all.at[block, (y + 1) % 4, core], y_left
        far_copies.append(send(here, here, far_sem, order, device))

    def twin_rows(order):
        far_copies[order].wait_recv()
        here = rows_all.at[blocks[order], :, core]
        twin_copies.append(send(here, here, twin_sem, order, twin))

    for order in range(4):
        pass_rows(order)
    pass_weight(0, up_first, up_direct)
    across.wait_recv()
    here = message_all.at[(1 - at.z_hi) * 4 + x]
    spread += [send(here, here, spread_sem, 3 + step, at.at_x(x + step)) for step in (1, 2, 3)]
    moved_rows.wait()
    for order in range(4, 8):
        pass_rows(order)
        twin_rows(order - 4)

    own = message_all[tensor].reshape(64, 2, 128)[:, 0, :].astype(BF16)
    tiled = []
    for first in (64, 96):
        tile = one_hot(iota((128, 256), 0) == first + iota((128, 256), 1) % 32)
        value = jnp.dot(own, tile, preferred_element_type=F32)
        keep = iota((64, 256), 1) // 32 == iota((64, 256), 0) % 8
        tiled.append(jnp.where(keep, value, 0.0).astype(BF16))

    @pl.loop(0, 8)
    def _(group):
        expand = one_hot(iota((64, 64), 1) == group * 8 + iota((64, 64), 0) // 8)
        slot, gate = (jnp.dot(expand, value, preferred_element_type=F32) for value in tiled)
        places, slots = iota((64, 256), 1), iota((64, 256), 0)
        match = (slot == (slots % 2 + 1).astype(F32)) & ((places // 8) % 4 == (slots // 2) % 4)
        pick[group] = one_hot(match)
        combine[group] = jnp.where(match, gate, 0.0).astype(BF16)

    for rr in range(2):
        for c in range(3):
            for b in range(4):
                k, n = iota((128, 128), 0), iota((128, 128), 1)
                here = (k - rr * 48 + b * 48 == c * 64 + n % 64) & (k >= rr * 48) & (k < rr * 48 + 48)
                order_map[b * 128 : b * 128 + 128, (rr * 3 + c) * 128 : (rr * 3 + c) * 128 + 128] = (
                    one_hot(here)
                )
    for order in range(4, 8):
        twin_rows(order)
    arrive(spread)

    @pl.loop(0, 8)
    def _(t):
        right_rows[...] = message_all[t].reshape(64, 2, 128)[:, 1, :]
        entries = jnp.concatenate(
            [right_rows[pl.ds(b, 16, stride=4), :] for b in range(4)], axis=1
        ).astype(BF16)
        placed = jnp.dot(entries, order_map[...], preferred_element_type=F32)
        for rr in range(2):
            for c in range(3):
                lanes = slice((rr * 3 + c) * 128, (rr * 3 + c) * 128 + 128)
                right_all[t * 2 + rr, pl.ds(c, 16, stride=3), :] = placed[:, lanes]

    arrive(up_direct[:4] + up_direct[6:], up_direct[4:6])
    down_first, down_direct = send_weight(1)

    widen = jnp.where(iota((8, 512), 1) // 64 == iota((8, 512), 0), 1.0, 0.0)

    @pl.loop(0, 8)
    def _(index):
        group, half = index // 2, index % 2
        left = message_all[at.z_hi * 4 + group, half * 4 + x].reshape(8, 2, 128)[:, 0, :]
        left_all[...] = contract_first(left, widen)
        for j in range(4):
            for lane in range(4):
                lanes = slice(lane * 128, lane * 128 + 128)
                delta = jnp.zeros((48, 128), F32)
                for r in range(16):
                    delta = delta + right_all[r] * left_all[j * 16 + r : j * 16 + r + 1, lanes]
                units = slice(j * 48, j * 48 + 48)
                weight[group, half, units, lanes] = (
                    up_all[half, group, units, lanes].astype(F32) + delta
                ).astype(BF16)

    pass_weight(1, down_first, down_direct)
    for order, block in enumerate(blocks):
        twin_copies[order].wait_recv()
    for group in range(8):
        value = jnp.dot(
            pick[group], rows_all[group].reshape(256, 1024), preferred_element_type=F32
        )
        picked[group * 64 : group * 64 + 64] = value.astype(BF16)

    def project(group):
        total = jnp.zeros((192, 512), F32)
        for half in (0, 1):
            total = total + lax.dot_general(
                weight[group, half], picked[:, half * 512 : half * 512 + 512],
                (((1,), (1,)), ((), ())), preferred_element_type=F32,
            )
        part[group] = total.astype(BF16)

    right_x, left_x, far_x = (x + 1) % 4, (x + 3) % 4, (x + 2) % 4
    top, low = pl.ds(0, 96), pl.ds(96, 96)
    project(far_x)
    copies = [
        send(part.at[far_x, top], hidden_far.at[0], hidden_sem, 0, x_right),
        send(part.at[far_x, low], hidden_far.at[1], hidden_sem, 1, x_left),
    ]
    project(right_x)
    copies.append(send(part.at[right_x, low], hidden_near.at[0, low], hidden_sem, 2, x_right))
    project(left_x)
    copies.append(send(part.at[left_x, top], hidden_near.at[1, top], hidden_sem, 3, x_left))
    copies[0].wait_recv()
    hidden_pass[0] = (part[right_x, top].astype(F32) + hidden_far[0].astype(F32)).astype(BF16)
    copies.append(send(hidden_pass.at[0], hidden_near.at[0, top], hidden_sem, 4, x_right))
    copies[1].wait_recv()
    hidden_pass[1] = (part[left_x, low].astype(F32) + hidden_far[1].astype(F32)).astype(BF16)
    copies.append(send(hidden_pass.at[1], hidden_near.at[1, low], hidden_sem, 5, x_left))
    project(x)
    arrive(copies[2:])
    value = part[x].astype(F32) + hidden_near[0].astype(F32) + hidden_near[1].astype(F32)
    hidden[x] = (value / (1.0 + jnp.exp(-value))).astype(BF16)
    here = hidden.at[x]
    from_left = send(here, here, gather_sem, 0, x_right)
    from_right = send(here, here, gather_sem, 1, x_left)
    from_left.wait_recv()
    here = hidden.at[left_x, top]
    far_top = send(here, here, gather_sem, 2, x_right)
    from_right.wait_recv()
    here = hidden.at[right_x, low]
    far_low = send(here, here, gather_sem, 3, x_left)
    arrive(down_direct[:4] + down_direct[6:], down_direct[4:6])
    arrive([far_top, far_low])

    order = [(y + 2) % 4, (y + 1) % 4, (y + 3) % 4, y]
    twins = {}
    for half in (0, 1):
        result = contract_first(
            hidden[...].reshape(768, 512), down_all[half].reshape(768, 512)
        ).astype(BF16)
        for group in range(8):
            value = contract_first(
                combine[group], result[group * 64 : group * 64 + 64]
            ).astype(BF16)
            for to_y in range(4):
                for to_core in range(2):
                    first = (to_y * 2 + to_core) * 32
                    mixed[to_core, to_y, half * 8 + group] = value[first : first + 32]
        zs = pl.ds(half * 8, 8)
        for i, to in enumerate(order):
            twins[i, half] = send(mixed.at[1 - core, to, zs], twin_in.at[to, zs],
                                  core_sem, half * 4 + i, twin)

    def sum_cores(i, half):
        to, base = order[i], half * 8
        twins[i, half].wait_recv()
        add_blocks(
            sums.at[i, pl.ds(base, 8)], 8,
            lambda k: mixed[core, to, base + k], lambda k: twin_in[to, base + k],
        )

    top, low = pl.ds(0, 8), pl.ds(8, 8)
    sum_cores(0, 0)
    copies = [send(sums.at[0, top], far.at[0], mix_far_sem, 0, y_right)]
    sum_cores(0, 1)
    copies.append(send(sums.at[0, low], far.at[1], mix_far_sem, 1, y_left))
    sum_cores(1, 1)
    copies.append(send(sums.at[1, low], near.at[0, low], mix_near_sem, 0, y_right))
    sum_cores(2, 0)
    copies.append(send(sums.at[2, top], near.at[1, top], mix_near_sem, 1, y_left))
    sum_cores(1, 0)
    sum_cores(2, 1)
    copies[0].wait_recv()
    add_blocks(sums.at[1], 8, lambda k: sums[1, k], lambda k: far[0, k])
    copies.append(send(sums.at[1, top], near.at[0, top], mix_near_sem, 2, y_right))
    copies[1].wait_recv()
    add_blocks(sums.at[2, low], 8, lambda k: sums[2, 8 + k], lambda k: far[1, k])
    copies.append(send(sums.at[2, low], near.at[1, low], mix_near_sem, 3, y_left))
    sum_cores(3, 0)
    sum_cores(3, 1)
    arrive(copies[2:])
    add_blocks(line, 16, lambda k: sums[3, k], lambda k: near[0, k], lambda k: near[1, k])

    rights, lefts = [], []
    for step in range(8):
        value = line[(z + 8 - step) % 16].astype(F32)
        if step > 0:
            rights[step - 1].wait_recv()
            value = value + right_in[step - 1].astype(F32)
        right_out[step] = value.astype(BF16)
        rights.append(send(right_out.at[step], right_in.at[step], right_sem, step, z_right))
        if step < 7:
            value = line[(z + 9 + step) % 16].astype(F32)
            if step > 0:
                lefts[step - 1].wait_recv()
                value = value + left_in[step - 1].astype(F32)
            left_out[step] = value.astype(BF16)
            lefts.append(send(left_out.at[step], left_in.at[step], left_sem, step, z_left))
    lefts[6].wait_recv()
    rights[7].wait_recv()
    value = line[z].astype(F32) + right_in[7].astype(F32) + left_in[6].astype(F32)
    out[...] = value.astype(BF16)
    for copy in unsent:
        copy.wait_send()


def layer(up, down, rows, message):
    any_space = pl.BlockSpec(memory_space=pl.ANY)
    return pl.pallas_call(
        layer_kernel,
        out_shape=jax.ShapeDtypeStruct((32, 512), BF16),
        in_specs=[any_space] * 4,
        out_specs=pl.BlockSpec(memory_space=pltpu.VMEM),
        scratch_shapes=[
            pltpu.VMEM((2, 4, 192, 512), BF16),
            pltpu.VMEM((2, 4, 192, 512), BF16),
            pltpu.VMEM((2, 2, 192, 512), BF16),
            pltpu.VMEM((8, 4, 2, 32, 1024), BF16),
            pltpu.VMEM((8, 4, 2, 2, 128), F32),
            pltpu.VMEM((8, 4, 2, 2, 128), F32),
            pltpu.VMEM((8, 8, 4, 2, 2, 128), F32),
            pltpu.VMEM((8, 64, 256), BF16),
            pltpu.VMEM((8, 64, 256), BF16),
            pltpu.VMEM((512, 768), BF16),
            pltpu.VMEM((64, 128), F32),
            pltpu.VMEM((16, 48, 128), F32),
            pltpu.VMEM((128, 512), F32),
            pltpu.VMEM((4, 2, 192, 512), BF16),
            pltpu.VMEM((512, 1024), BF16),
            pltpu.VMEM((4, 192, 512), BF16),
            pltpu.VMEM((2, 96, 512), BF16),
            pltpu.VMEM((2, 192, 512), BF16),
            pltpu.VMEM((2, 96, 512), BF16),
            pltpu.VMEM((4, 192, 512), BF16),
            pltpu.VMEM((2, 4, 16, 32, 512), BF16),
            pltpu.VMEM((4, 16, 32, 512), BF16),
            pltpu.VMEM((4, 16, 32, 512), BF16),
            pltpu.VMEM((2, 8, 32, 512), BF16),
            pltpu.VMEM((2, 16, 32, 512), BF16),
            pltpu.VMEM((16, 32, 512), BF16),
            pltpu.VMEM((8, 32, 512), BF16),
            pltpu.VMEM((7, 32, 512), BF16),
            pltpu.VMEM((8, 32, 512), BF16),
            pltpu.VMEM((7, 32, 512), BF16),
            pltpu.SemaphoreType.DMA((8,)),
            dma_sems(7),
            dma_sems(16),
            dma_sems(8),
            dma_sems(8),
            dma_sems(8),
            dma_sems(8),
            dma_sems(11),
            dma_sems(7),
            dma_sems(6),
            dma_sems(4),
            dma_sems(8),
            dma_sems(2),
            dma_sems(4),
            dma_sems(8),
            dma_sems(7),
        ],
        compiler_params=pltpu.CompilerParams(
            collective_id=0, has_side_effects=True, vmem_limit_bytes=VMEM_LIMIT
        ),
        name="layer",
    )(up, down, rows, message)


def body(
    core_left,
    core_right,
    grad_left,
    grad_right,
    first_left,
    first_right,
    second_left,
    second_right,
    up_base,
    down_base,
    states,
    routes,
    gates,
):
    left_next, first_left_next, second_left_next = adamw_update(
        core_left, grad_left, first_left, second_left
    )
    right_next, first_right_next, second_right_next = adamw_update(
        core_right, grad_right, first_right, second_right
    )
    chosen = (routes[..., None] == jnp.arange(64, dtype=jnp.int32)).astype(F32)
    taken = jnp.sum(chosen, axis=2)
    weight = jnp.sum(chosen * gates[..., None], axis=2)
    earlier = jnp.cumsum(taken, axis=1) - taken
    slot = taken * (earlier + 1.0)
    message = jnp.concatenate(
        [
            lax.reduce_precision(left_next, 8, 7).reshape(64, 64),
            slot.reshape(32, 64),
            weight.reshape(32, 64),
            lax.reduce_precision(right_next, 8, 7).reshape(96, 64),
            jnp.zeros((32, 64), F32),
        ],
        axis=0,
    )
    message = message.T.reshape(8, 4, 2, 2, 128)
    x = lax.axis_index("tensor") % 4
    rows = lax.dynamic_index_in_dim(states.reshape(32, 2, 4, 512), x, 2, keepdims=False)
    mixed = layer(up_base[0], down_base[0], rows.reshape(32, 1024), message)
    mixed = mixed.reshape(4, 8, 512)
    return (
        mixed,
        left_next,
        right_next,
        first_left_next,
        first_right_next,
        second_left_next,
        second_right_next,
    )


def solution(mesh):
    cores = (P("tensor", "train"),) * 6
    in_specs = cores + (P("tensor", "train"),) * 2 + (
        P("train", "tensor", None),
        P("train", "tensor", None),
        P(None, "train", None),
        P(None, "train", None),
        P(None, "train", None),
    )
    out_specs = (P(None, "train", "tensor"),) + cores
    return jax.shard_map(body, mesh=mesh, in_specs=in_specs, out_specs=out_specs, check_vma=False)
```

time: 968 us -> 142 us (0.15)
  waiting for transfers between devices: 495 us -> 0 us
  blocking collectives: 330 us -> 0 us
  Pallas kernels: 0 us -> 133 us
  starting transfers between devices: 58.5 us -> 0 us
  local copies, waits for them, and re-layouts: 35.1 us -> 4.04 us
  matrix products: 25.1 us -> 0 us
  between operations: 14.1 us -> 0.75 us
    reduce_scatter x4 -> x0, waiting for transfers between devices: 372 us -> none  [body(): lax.psum_scatter(partial_out.astype(jnp.bfloat16), 'tensor', scatter_dime...]
    all_gather x3 -> x0, blocking collectives: 330 us -> none  [the longest x1 134 us: body(): lax.all_gather(right_split, 'train', axis=1, tiled=True)]
    pallas_call x0 -> x1, Pallas kernels: none -> 133 us  [layer(): pl.pallas_call(layer_kernel, out_shape=jax.ShapeDtypeStruct((32, 512), BF...]
    all_to_all x8 -> x0, waiting for transfers between devices: 123 us -> none  [the longest x4 109 us: body(): lax.all_to_all(buffer, 'train', split_axis=0, concat_axis=0, tiled=True)]
    all_to_all x8 -> x0, starting transfers between devices: 58.1 us -> none  [the longest x4 35.6 us: body(): lax.all_to_all(buffer, 'train', split_axis=0, concat_axis=0, tiled=True)]
    dot_general x13 -> x0, matrix products: 25.1 us -> none  [the longest x4 16 us: body(): jnp.einsum('scf,fd->scd', hidden, down_local, preferred_element_type=jnp....]
    reshape x14 -> x4, local copies, waits for them, and re-layouts: 14.6 us -> 1.47 us  [the longest x1 1.25 us: body(): states.reshape(32, 2, 4, 512)]
  transfers between devices with their start and end apart: 12 -> 0, of which waited for: 7 -> 0; matrix products, arithmetic and copies ran while one was open for 6% -> 0% of each run, Pallas kernels for 0% -> 0%
where the time goes in v2:
time: 142 us
  Pallas kernels  133 us (94%)
  local copies, waits for them, and re-layouts  4.04 us (3%)
  other arithmetic  3.85 us (3%)
    pallas_call x1, Pallas kernels, layer(): pl.pallas_call(layer_kernel, out_shape=jax.ShapeDtypeStruct((32, 512), BF...  133 us

profile of v2, /device:TPU:6, one launch (start us, length us, event | category | flops | bytes accessed | tf_op | source)
XLA Modules:
  0.0 141.6 jit_solution(3439537197309937370)
XLA Ops:
  0.6 0.0 copy-start
  0.7 1.3 reshape.41
  1.9 0.4 dynamic-slice_reduce_fusion
  2.4 1.4 %fusion.7 = (f32[4,1024]{1,0:T(4,128)S(1)}, f32[4,1024]{1,0:T(4,128)}, f32[4,1024]{1,0:T(4,128)}, f32[4,1024]{1,0:T(4,128)}) fusion(f32[4,1024]{1,0:T(4,128)} %param.13, f32[4,1024]{1,0:T(4,128)} %param.15, f32[4,1024]{1,0:T(4,128)} %param.17, f32[4,1024]{1,0:T(4,128)} %param.19), kind=kLoop, calls=%fused_computation.21 | loop fusion | flops 65536 | bytes 131072 | tf_op jit(solution)/shard_map/reduce_precision | solution.py:536
  3.8 0.1 reshape.43
  3.9 0.9 select_reduce_fusion
  4.8 1.5 %fusion.5 = (f32[2,3072]{1,0:T(2,128)S(1)}, f32[2,3072]{1,0:T(2,128)}, f32[2,3072]{1,0:T(2,128)}, f32[2,3072]{1,0:T(2,128)}) fusion(f32[2,3072]{1,0:T(2,128)} %param.14, f32[2,3072]{1,0:T(2,128)} %param.16, f32[2,3072]{1,0:T(2,128)} %param.18, f32[2,3072]{1,0:T(2,128)} %param.20), kind=kLoop, calls=%fused_computation.20 | loop fusion | flops 98304 | bytes 196608 | tf_op jit(solution)/shard_map/reduce_precision | solution.py:539
  6.3 0.1 reshape.45
  6.5 0.1 copy.26
  6.6 0.0 copy-done
  6.6 0.0 copy-start.1
  6.6 1.4 copy-done.1
  8.0 132.9 %layer.1 = bf16[32,512]{1,0:T(8,128)(2,1)S(1)} custom-call(bf16[192,4096]{1,0:T(8,128)(2,1)S(1)} %bitcast.18, bf16[192,4096]{1,0:T(8,128)(2,1)S(1)} %bitcast.19, bf16[32,1024]{1,0:T(8,128)(2,1)S(1)} %bitcast.20, f32[8,4,2,2,128]{4,3,2,1,0:T(2,128)S(1)} %reshape.46.message), custom_call_target="tpu_custom_call" | custom-call | tf_op jit(solution)/shard_map/layer/pallas_call | solution.py:448
  140.9 0.6 copy.34
  (8 shorter events, 0.1 us)
Async XLA Ops:
  0.6 6.0 %copy-start = (bf16[1,192,4096]{2,1,0:T(8,128)(2,1)S(1)}, bf16[1,192,4096]{2,1,0:T(8,128)(2,1)}, u32[]{:S(2)}) copy-start(bf16[1,192,4096]{2,1,0:T(8,128)(2,1)} %param.21) | copy-start | bytes 4718596
  6.6 1.4 copy-start.1

commit v3 on v2

--- a/solution.py
+++ b/solution.py
@@ -16,7 +16,7 @@
 EPSILON = 1e-08
 STEP_NUMBER = 10.0
 
-VMEM_LIMIT = 48 * 1024 * 1024
+VMEM_LIMIT = 60 * 1024 * 1024
 
 
 def adamw_update(value_now, gradient, first_moment, second_moment):
@@ -92,24 +92,15 @@
     return lax.dot_general(left, right, (((0,), (0,)), ((), ())), preferred_element_type=F32)
 
 
-def add_blocks(dst, count, *terms):
-    @pl.loop(0, count)
-    def _(i):
-        total = terms[0](i).astype(F32)
-        for term in terms[1:]:
-            total = total + term(i).astype(F32)
-        dst[i] = total.astype(BF16)
-
-
 def layer_kernel(
     up, down, rows, message, out,
     up_all, down_all, relay, rows_all, message_z, message_y, message_all,
-    pick, combine, order_map, right_rows, right_all, left_all, weight, picked,
+    pick, combine, order_map, right_rows, entries, right_all, left_all, weight, picked,
     part, hidden_far, hidden_near, hidden_pass, hidden,
-    mixed, twin_in, sums, far, near, line, right_in, left_in, right_out, left_out,
+    result, twin_in, slots_in, slots_relay, line, right_in, left_in, right_out, left_out,
     local_sem, z_sem, y_sem, far_sem, twin_sem, weight_sem, relay_sem,
     message_sem, spread_sem, hidden_sem, gather_sem,
-    core_sem, mix_far_sem, mix_near_sem, right_sem, left_sem,
+    core_sem, slots_sem, slots_relay_sem, right_sem, left_sem,
 ):
     at = Place()
     tensor, x, y, z_lo, z, core = at.tensor, at.x, at.y, at.z_lo, at.z, at.core
@@ -253,27 +244,49 @@
     across.wait_recv()
     here = message_all.at[(1 - at.z_hi) * 4 + x]
     spread += [send(here, here, spread_sem, 3 + step, at.at_x(x + step)) for step in (1, 2, 3)]
+    down_first, down_direct = send_weight(1)
     moved_rows.wait()
     for order in range(4, 8):
         pass_rows(order)
         twin_rows(order - 4)
 
+    def spread_rows(messages, first, count):
+        tile = one_hot(iota((128, count), 0) == first + iota((128, count), 1) % 32)
+        return jnp.dot(messages, tile, preferred_element_type=F32).astype(BF16)
+
     own = message_all[tensor].reshape(64, 2, 128)[:, 0, :].astype(BF16)
-    tiled = []
-    for first in (64, 96):
-        tile = one_hot(iota((128, 256), 0) == first + iota((128, 256), 1) % 32)
-        value = jnp.dot(own, tile, preferred_element_type=F32)
-        keep = iota((64, 256), 1) // 32 == iota((64, 256), 0) % 8
-        tiled.append(jnp.where(keep, value, 0.0).astype(BF16))
+    codes = spread_rows(own, 64, 512)
+
+    @pl.loop(0, 4)
+    def _(pair):
+        slots, source = iota((128, 64), 0), iota((128, 64), 1)
+        expand = one_hot(source == (pair * 2 + (slots // 8) % 2) * 8 + slots // 16)
+        code = jnp.dot(expand, codes, preferred_element_type=F32)
+        slots, places = iota((128, 512), 0), iota((128, 512), 1)
+        match = (
+            (code == (slots % 2 + 1).astype(F32))
+            & (places // 256 == (slots // 8) % 2)
+            & ((places // 32) % 8 == slots // 16)
+            & ((places // 8) % 4 == (slots // 2) % 4)
+        )
+        pick[pair] = one_hot(match)
+
+    passed = message_z[...].reshape(64, 2, 128)[:, 0, :].astype(BF16)
+    codes, gates = spread_rows(passed, 64, 256), spread_rows(passed, 96, 256)
 
     @pl.loop(0, 8)
-    def _(group):
-        expand = one_hot(iota((64, 64), 1) == group * 8 + iota((64, 64), 0) // 8)
-        slot, gate = (jnp.dot(expand, value, preferred_element_type=F32) for value in tiled)
-        places, slots = iota((64, 256), 1), iota((64, 256), 0)
-        match = (slot == (slots % 2 + 1).astype(F32)) & ((places // 8) % 4 == (slots // 2) % 4)
-        pick[group] = one_hot(match)
-        combine[group] = jnp.where(match, gate, 0.0).astype(BF16)
+    def _(expert):
+        slots, source = iota((64, 64), 0), iota((64, 64), 1)
+        expand = one_hot(source == (slots // 8) * 8 + expert)
+        code = jnp.dot(expand, codes, preferred_element_type=F32)
+        gate = jnp.dot(expand, gates, preferred_element_type=F32)
+        slots, places = iota((64, 256), 0), iota((64, 256), 1)
+        match = (
+            (code == (slots % 2 + 1).astype(F32))
+            & (places // 32 == slots // 8)
+            & ((places // 8) % 4 == (slots // 2) % 4)
+        )
+        combine[expert] = jnp.where(match, gate, 0.0).astype(BF16)
 
     for rr in range(2):
         for c in range(3):
@@ -287,20 +300,21 @@
         twin_rows(order)
     arrive(spread)
 
-    @pl.loop(0, 8)
-    def _(t):
-        right_rows[...] = message_all[t].reshape(64, 2, 128)[:, 1, :]
-        entries = jnp.concatenate(
-            [right_rows[pl.ds(b, 16, stride=4), :] for b in range(4)], axis=1
+    for t in range(8):
+        right_rows[t] = message_all[t].reshape(64, 2, 128)[:, 1, :]
+        entries[t * 16 : t * 16 + 16] = jnp.concatenate(
+            [right_rows[t, pl.ds(b, 16, stride=4), :] for b in range(4)], axis=1
         ).astype(BF16)
-        placed = jnp.dot(entries, order_map[...], preferred_element_type=F32)
+    placed = jnp.dot(entries[...], order_map[...], preferred_element_type=F32)
+    for t in range(8):
         for rr in range(2):
             for c in range(3):
                 lanes = slice((rr * 3 + c) * 128, (rr * 3 + c) * 128 + 128)
-                right_all[t * 2 + rr, pl.ds(c, 16, stride=3), :] = placed[:, lanes]
+                right_all[t * 2 + rr, pl.ds(c, 16, stride=3), :] = (
+                    placed[t * 16 : t * 16 + 16, lanes]
+                )
 
     arrive(up_direct[:4] + up_direct[6:], up_direct[4:6])
-    down_first, down_direct = send_weight(1)
 
     widen = jnp.where(iota((8, 512), 1) // 64 == iota((8, 512), 0), 1.0, 0.0)
 
@@ -323,11 +337,14 @@
     pass_weight(1, down_first, down_direct)
     for order, block in enumerate(blocks):
         twin_copies[order].wait_recv()
-    for group in range(8):
+    for pair in range(4):
         value = jnp.dot(
-            pick[group], rows_all[group].reshape(256, 1024), preferred_element_type=F32
-        )
-        picked[group * 64 : group * 64 + 64] = value.astype(BF16)
+            pick[pair],
+            rows_all[pair * 2 : pair * 2 + 2].reshape(512, 1024),
+            preferred_element_type=F32,
+        ).astype(BF16)
+        for group in range(8):
+            picked[pl.ds(group * 64 + pair * 16, 16), :] = value[group * 16 : group * 16 + 16]
 
     def project(group):
         total = jnp.zeros((192, 512), F32)
@@ -371,65 +388,68 @@
     arrive(down_direct[:4] + down_direct[6:], down_direct[4:6])
     arrive([far_top, far_low])
 
-    order = [(y + 2) % 4, (y + 1) % 4, (y + 3) % 4, y]
-    twins = {}
+    right_y, left_y, far_y = (y + 1) % 4, (y + 3) % 4, (y + 2) % 4
+    twins, direct, relayed, own_slots = [], [], [], []
     for half in (0, 1):
-        result = contract_first(
-            hidden[...].reshape(768, 512), down_all[half].reshape(768, 512)
-        ).astype(BF16)
+        result[half] = (
+            contract_first(hidden[...].reshape(768, 512), down_all[half].reshape(768, 512))
+            .astype(BF16)
+            .reshape(4, 2, 64, 512)
+        )
+        twins.append(send(result.at[half, :, 1 - core], twin_in.at[half], core_sem, half, twin))
+        relayed.append(
+            send(result.at[half, far_y, core], slots_relay.at[half, 0],
+                 slots_relay_sem, half, y_right)
+        )
+        here = slots_in.at[half, y, core]
+        direct.append(send(result.at[half, right_y, core], here, slots_sem, half * 2, y_right))
+        direct.append(send(result.at[half, left_y, core], here, slots_sem, half * 2 + 1, y_left))
+        own_slots.append(move(result.at[half, y, core], here, 8 + half))
+    for half in (0, 1):
+        twins[half].wait_recv()
+        relayed.append(
+            send(twin_in.at[half, far_y], slots_relay.at[half, 1],
+                 slots_relay_sem, 2 + half, y_left)
+        )
+        here = slots_in.at[half, y, 1 - core]
+        direct.append(send(twin_in.at[half, right_y], here, slots_sem, 4 + half * 2, y_right))
+        direct.append(send(twin_in.at[half, left_y], here, slots_sem, 5 + half * 2, y_left))
+        own_slots.append(move(twin_in.at[half, y], here, 10 + half))
+    onward = []
+    for half in (0, 1):
+        relayed[half].wait_recv()
+        onward.append(
+            send(slots_relay.at[half, 0], slots_in.at[half, left_y, core],
+                 slots_relay_sem, 4 + half, y_right)
+        )
+    for half in (0, 1):
+        relayed[2 + half].wait_recv()
+        onward.append(
+            send(slots_relay.at[half, 1], slots_in.at[half, right_y, 1 - core],
+                 slots_relay_sem, 6 + half, y_left)
+        )
+    for half in (0, 1):
+        arrive(
+            [direct[half * 2], direct[half * 2 + 1], direct[4 + half * 2], direct[5 + half * 2]]
+            + [onward[half], onward[2 + half]],
+            [own_slots[half], own_slots[2 + half]],
+        )
+        value = contract_first(
+            combine[...].reshape(512, 256), slots_in[half].reshape(512, 512)
+        )
         for group in range(8):
-            value = contract_first(
-                combine[group], result[group * 64 : group * 64 + 64]
-            ).astype(BF16)
-            for to_y in range(4):
-                for to_core in range(2):
-                    first = (to_y * 2 + to_core) * 32
-                    mixed[to_core, to_y, half * 8 + group] = value[first : first + 32]
-        zs = pl.ds(half * 8, 8)
-        for i, to in enumerate(order):
-            twins[i, half] = send(mixed.at[1 - core, to, zs], twin_in.at[to, zs],
-                                  core_sem, half * 4 + i, twin)
-
-    def sum_cores(i, half):
-        to, base = order[i], half * 8
-        twins[i, half].wait_recv()
-        add_blocks(
-            sums.at[i, pl.ds(base, 8)], 8,
-            lambda k: mixed[core, to, base + k], lambda k: twin_in[to, base + k],
-        )
-
-    top, low = pl.ds(0, 8), pl.ds(8, 8)
-    sum_cores(0, 0)
-    copies = [send(sums.at[0, top], far.at[0], mix_far_sem, 0, y_right)]
-    sum_cores(0, 1)
-    copies.append(send(sums.at[0, low], far.at[1], mix_far_sem, 1, y_left))
-    sum_cores(1, 1)
-    copies.append(send(sums.at[1, low], near.at[0, low], mix_near_sem, 0, y_right))
-    sum_cores(2, 0)
-    copies.append(send(sums.at[2, top], near.at[1, top], mix_near_sem, 1, y_left))
-    sum_cores(1, 0)
-    sum_cores(2, 1)
-    copies[0].wait_recv()
-    add_blocks(sums.at[1], 8, lambda k: sums[1, k], lambda k: far[0, k])
-    copies.append(send(sums.at[1, top], near.at[0, top], mix_near_sem, 2, y_right))
-    copies[1].wait_recv()
-    add_blocks(sums.at[2, low], 8, lambda k: sums[2, 8 + k], lambda k: far[1, k])
-    copies.append(send(sums.at[2, low], near.at[1, low], mix_near_sem, 3, y_left))
-    sum_cores(3, 0)
-    sum_cores(3, 1)
-    arrive(copies[2:])
-    add_blocks(line, 16, lambda k: sums[3, k], lambda k: near[0, k], lambda k: near[1, k])
+            line[half * 8 + group] = value[group * 32 : group * 32 + 32]
 
     rights, lefts = [], []
     for step in range(8):
-        value = line[(z + 8 - step) % 16].astype(F32)
+        value = line[(z + 8 - step) % 16]
         if step > 0:
             rights[step - 1].wait_recv()
             value = value + right_in[step - 1].astype(F32)
         right_out[step] = value.astype(BF16)
         rights.append(send(right_out.at[step], right_in.at[step], right_sem, step, z_right))
         if step < 7:
-            value = line[(z + 9 + step) % 16].astype(F32)
+            value = line[(z + 9 + step) % 16]
             if step > 0:
                 lefts[step - 1].wait_recv()
                 value = value + left_in[step - 1].astype(F32)
@@ -437,7 +457,7 @@
             lefts.append(send(left_out.at[step], left_in.at[step], left_sem, step, z_left))
     lefts[6].wait_recv()
     rights[7].wait_recv()
-    value = line[z].astype(F32) + right_in[7].astype(F32) + left_in[6].astype(F32)
+    value = line[z] + right_in[7].astype(F32) + left_in[6].astype(F32)
     out[...] = value.astype(BF16)
     for copy in unsent:
         copy.wait_send()
@@ -458,10 +478,11 @@
             pltpu.VMEM((8, 4, 2, 2, 128), F32),
             pltpu.VMEM((8, 4, 2, 2, 128), F32),
             pltpu.VMEM((8, 8, 4, 2, 2, 128), F32),
-            pltpu.VMEM((8, 64, 256), BF16),
+            pltpu.VMEM((4, 128, 512), BF16),
             pltpu.VMEM((8, 64, 256), BF16),
             pltpu.VMEM((512, 768), BF16),
-            pltpu.VMEM((64, 128), F32),
+            pltpu.VMEM((8, 64, 128), F32),
+            pltpu.VMEM((128, 512), BF16),
             pltpu.VMEM((16, 48, 128), F32),
             pltpu.VMEM((128, 512), F32),
             pltpu.VMEM((4, 2, 192, 512), BF16),
@@ -471,17 +492,16 @@
             pltpu.VMEM((2, 192, 512), BF16),
             pltpu.VMEM((2, 96, 512), BF16),
             pltpu.VMEM((4, 192, 512), BF16),
-            pltpu.VMEM((2, 4, 16, 32, 512), BF16),
-            pltpu.VMEM((4, 16, 32, 512), BF16),
-            pltpu.VMEM((4, 16, 32, 512), BF16),
-            pltpu.VMEM((2, 8, 32, 512), BF16),
-            pltpu.VMEM((2, 16, 32, 512), BF16),
-            pltpu.VMEM((16, 32, 512), BF16),
+            pltpu.VMEM((2, 4, 2, 64, 512), BF16),
+            pltpu.VMEM((2, 4, 64, 512), BF16),
+            pltpu.VMEM((2, 4, 2, 64, 512), BF16),
+            pltpu.VMEM((2, 2, 64, 512), BF16),
+            pltpu.VMEM((16, 32, 512), F32),
             pltpu.VMEM((8, 32, 512), BF16),
             pltpu.VMEM((7, 32, 512), BF16),
             pltpu.VMEM((8, 32, 512), BF16),
             pltpu.VMEM((7, 32, 512), BF16),
-            pltpu.SemaphoreType.DMA((8,)),
+            pltpu.SemaphoreType.DMA((12,)),
             dma_sems(7),
             dma_sems(16),
             dma_sems(8),
@@ -492,9 +512,9 @@
             dma_sems(7),
             dma_sems(6),
             dma_sems(4),
-            dma_sems(8),
             dma_sems(2),
-            dma_sems(4),
+            dma_sems(8),
+            dma_sems(8),
             dma_sems(8),
             dma_sems(7),
         ],

time: 142 us -> 129 us (0.908)
  Pallas kernels: 133 us -> 120 us
    pallas_call x1, Pallas kernels: 133 us -> 120 us  [layer(): pl.pallas_call(layer_kernel, out_shape=jax.ShapeDtypeStruct((32, 512), BF...]
where the time goes in v3:
time: 129 us
  Pallas kernels  120 us (93%)
  local copies, waits for them, and re-layouts  4.51 us (3%)
  other arithmetic  3.84 us (3%)
    pallas_call x1, Pallas kernels, layer(): pl.pallas_call(layer_kernel, out_shape=jax.ShapeDtypeStruct((32, 512), BF...  120 us

profile of v3, /device:TPU:6, one launch (start us, length us, event | category | flops | bytes accessed | tf_op | source)
XLA Modules:
  0.0 128.7 jit_solution(904560963544863422)
XLA Ops:
  0.6 1.1 reshape.41
  1.8 0.4 dynamic-slice_reduce_fusion
  2.2 0.6 copy.28
  2.9 1.4 %fusion.7 = (f32[4,1024]{1,0:T(4,128)S(1)}, f32[4,1024]{1,0:T(4,128)}, f32[4,1024]{1,0:T(4,128)}, f32[4,1024]{1,0:T(4,128)}) fusion(f32[4,1024]{1,0:T(4,128)} %param.13, f32[4,1024]{1,0:T(4,128)} %param.15, f32[4,1024]{1,0:T(4,128)} %param.17, f32[4,1024]{1,0:T(4,128)} %param.19), kind=kLoop, calls=%fused_computation.21 | loop fusion | flops 65536 | bytes 131072 | tf_op jit(solution)/shard_map/reduce_precision | solution.py:556
  4.3 0.1 reshape.43
  4.4 0.9 select_reduce_fusion
  5.3 1.5 %fusion.5 = (f32[2,3072]{1,0:T(2,128)S(1)}, f32[2,3072]{1,0:T(2,128)}, f32[2,3072]{1,0:T(2,128)}, f32[2,3072]{1,0:T(2,128)}) fusion(f32[2,3072]{1,0:T(2,128)} %param.14, f32[2,3072]{1,0:T(2,128)} %param.16, f32[2,3072]{1,0:T(2,128)} %param.18, f32[2,3072]{1,0:T(2,128)} %param.20), kind=kLoop, calls=%fused_computation.20 | loop fusion | flops 98304 | bytes 196608 | tf_op jit(solution)/shard_map/reduce_precision | solution.py:559
  6.8 0.1 reshape.45
  6.9 0.1 copy.26
  7.0 0.7 reshape.46.message
  7.7 119.7 %layer.1 = bf16[32,512]{1,0:T(8,128)(2,1)} custom-call(bf16[192,4096]{1,0:T(8,128)(2,1)} %bitcast.18, bf16[192,4096]{1,0:T(8,128)(2,1)} %bitcast.19, bf16[32,1024]{1,0:T(8,128)(2,1)} %bitcast.20, f32[8,4,2,2,128]{4,3,2,1,0:T(2,128)} %reshape.46.message), custom_call_target="tpu_custom_call" | custom-call | tf_op jit(solution)/shard_map/layer/pallas_call | solution.py:468
  127.3 1.4 %copy.34 = bf16[4,8,512]{2,1,0:T(8,128)(2,1)} copy(bf16[4,8,512]{2,1,0:T(8,128)(2,1)} %bitcast.23) | data formatting | bytes 65536
  (6 shorter events, 0.1 us)

commit v4 on v3

--- a/solution.py
+++ b/solution.py
@@ -27,6 +27,57 @@
     update = first_next / first_scale / (jnp.sqrt(second_next / second_scale) + EPSILON)
     value_next = value_now - LEARN_RATE * (update + WEIGHT_DECAY * value_now)
     return (value_next, first_next, second_next)
+
+
+def prepare_kernel(
+    core_left, core_right, grad_left, grad_right, first_left, first_right, second_left, second_right,
+    routes, gates,
+    left_next, right_next, first_left_next, first_right_next, second_left_next, second_right_next,
+    message, entries,
+):
+    left, first, second = adamw_update(
+        core_left[...], grad_left[...], first_left[...], second_left[...]
+    )
+    left_next[...], first_left_next[...], second_left_next[...] = left, first, second
+    right, first, second = adamw_update(
+        core_right[...], grad_right[...], first_right[...], second_right[...]
+    )
+    right_next[...], first_right_next[...], second_right_next[...] = right, first, second
+
+    for r in range(16):
+        entries[0, r * 4 : r * 4 + 4] = left[:, r * 64 : r * 64 + 64]
+    for pair in range(48):
+        entries[1, pair * 2 : pair * 2 + 2] = right[:, pair * 64 : pair * 64 + 64]
+    entries[1, 96:128] = jnp.zeros((32, 64), F32)
+    expert = lax.broadcasted_iota(jnp.int32, (32, 64), 1)
+    taken, weight = jnp.zeros((32, 64), F32), jnp.zeros((32, 64), F32)
+    for k in range(8):
+        chosen = routes[:, k : k + 1] == expert
+        taken = taken + jnp.where(chosen, 1.0, 0.0)
+        weight = weight + jnp.where(chosen, gates[:, k : k + 1], 0.0)
+    to, by = (lax.broadcasted_iota(jnp.int32, (32, 32), dim) for dim in (0, 1))
+    before = jnp.where((by < to) & (by // 8 == to // 8), 1.0, 0.0)
+    earlier = jnp.dot(before, taken, preferred_element_type=F32)
+    entries[0, 64:96] = taken * (earlier + 1.0)
+    entries[0, 96:128] = weight
+    row, column = (lax.broadcasted_iota(jnp.int32, (128, 128), dim) for dim in (0, 1))
+    same = jnp.where(row == column, 1.0, 0.0).astype(BF16)
+    for kind in range(2):
+        message[:, kind, :] = lax.dot_general(
+            entries[kind].astype(BF16), same, (((0,), (0,)), ((), ())), preferred_element_type=F32
+        )
+
+
+def prepare(cores, routes, gates):
+    return pl.pallas_call(
+        prepare_kernel,
+        out_shape=(
+            *(jax.ShapeDtypeStruct(shape, F32) for shape in ((4, 1024), (2, 3072)) * 3),
+            jax.ShapeDtypeStruct((64, 2, 128), F32),
+        ),
+        scratch_shapes=[pltpu.VMEM((2, 128, 64), F32)],
+        name="prepare",
+    )(*cores, routes, gates)
 
 
 class Place:
@@ -50,6 +101,9 @@
     def at_x(self, x):
         return (self.train, self.z_hi * 4 + (x + 4) % 4)
 
+    def across_y(self, y):
+        return (self.z_lo * 8 + ((y + 4) % 4) * 2 + 1 - self.core, self.tensor)
+
     def twin(self):
         return (self.train + 1 - 2 * self.core, self.tensor)
 
@@ -94,11 +148,11 @@
 
 def layer_kernel(
     up, down, rows, message, out,
-    up_all, down_all, relay, rows_all, message_z, message_y, message_all,
+    up_all, down_all, relay, rows_z, slots_out, rows_relay, message_z, message_y, message_all,
     pick, combine, order_map, right_rows, entries, right_all, left_all, weight, picked,
     part, hidden_far, hidden_near, hidden_pass, hidden,
     result, twin_in, slots_in, slots_relay, line, right_in, left_in, right_out, left_out,
-    local_sem, z_sem, y_sem, far_sem, twin_sem, weight_sem, relay_sem,
+    local_sem, z_sem, y_sem, rows_relay_sem, twin_sem, weight_sem, relay_sem,
     message_sem, spread_sem, hidden_sem, gather_sem,
     core_sem, slots_sem, slots_relay_sem, right_sem, left_sem,
 ):
@@ -119,7 +173,9 @@
         signal(at.at_y(y + step))
     for device in (twin, z_right, z_left, at.other_half()):
         signal(device)
-    pl.semaphore_wait(pltpu.get_barrier_semaphore(), 17)
+    signal(at.across_y(y + 1))
+    signal(at.across_y(y - 1))
+    pl.semaphore_wait(pltpu.get_barrier_semaphore(), 19)
 
     unsent = []
 
@@ -133,23 +189,28 @@
         copy.start()
         return copy
 
-    here = rows_all.at[z_lo, y, core]
-    z_rights = [send(rows, here, z_sem, 0, z_right)]
-    z_lefts = [send(rows, here, z_sem, 4, z_left)]
+    def columns_of(half, to):
+        return pl.ds(pl.multiple_of((half * 4 + to) * 512, 512), 512)
+
+    halves = [
+        (rows.at[:, columns_of(half, x)], pl.ds(half * 512, 512)) for half in (0, 1)
+    ]
+    z_rights, z_lefts = [], []
+    for half, (origin, lanes) in enumerate(halves):
+        z_rights.append(send(origin, rows_z.at[1, :, lanes], z_sem, half, z_right))
+        z_lefts.append(send(origin, rows_z.at[2, :, lanes], z_sem, 2 + half, z_left))
+    moved_rows = [
+        move(origin, rows_z.at[0, :, lanes], half * 11 + 1)
+        for half, (origin, lanes) in enumerate(halves)
+    ]
 
     moved_z = move(message.at[z_lo], message_z.at[z_lo], 0)
     by_z = [
         send(message.at[(z_lo + step) % 8], message_z.at[z_lo], message_sem, step, same_half(step))
         for step in range(1, 8)
     ]
-    y_rights = [send(rows, here, y_sem, 0, y_right)]
-    y_lefts = [send(rows, here, y_sem, 8, y_left)]
-    moved_rows = move(rows, here, 1)
 
     weights = ((up, up_all), (down, down_all))
-
-    def columns_of(half, to):
-        return pl.ds(pl.multiple_of((half * 4 + to) * 512, 512), 512)
 
     def send_weight(w):
         origin, dst = weights[w]
@@ -188,90 +249,117 @@
     blocks = [z_lo]
     for order in range(1, 8):
         step = (order + 1) // 2
-        if order % 2 == 1:
-            z_rights[step - 1].wait_recv()
-            block = (z_lo - step + 8) % 8
-            here = rows_all.at[block, y, core]
-            if step < 4:
-                z_rights.append(send(here, here, z_sem, step, z_right))
+        blocks.append((z_lo - step + 8) % 8 if order % 2 == 1 else (z_lo + step) % 8)
+
+    def next_rows(order):
+        if order == 1:
+            arrive(z_rights[:2])
+        elif order == 2:
+            arrive(z_lefts[:2])
+        elif order % 2 == 1:
+            z_rights[order // 2 + 1].wait_recv()
         else:
-            z_lefts[step - 1].wait_recv()
-            block = (z_lo + step) % 8
-            here = rows_all.at[block, y, core]
-            if step < 3:
-                z_lefts.append(send(here, here, z_sem, 4 + step, z_left))
-        blocks.append(block)
-        y_rights.append(send(here, here, y_sem, order, y_right))
-        y_lefts.append(send(here, here, y_sem, 8 + order, y_left))
-        if order == 3:
-            arrive(by_z, [moved_z])
-            moved_y = move(message_z.at[:, y], message_y.at[:, y], 6)
-            by_y = [
-                send(message_z.at[:, (y + step) % 4], message_y.at[:, y],
-                     message_sem, 7 + step, at.at_y(y + step))
-                for step in (1, 2, 3)
-            ]
-        if order == 5:
-            arrive(by_y, [moved_y])
-            moved_core = move(message_y.at[:, :, core], message_all.at[tensor, :, :, core], 7)
-            by_core = send(message_y.at[:, :, 1 - core], message_all.at[tensor, :, :, core],
-                           message_sem, 0, twin)
-
+            z_lefts[order // 2].wait_recv()
+        here = rows_z.at[order]
+        if order in (1, 3, 5):
+            z_rights.append(send(here, rows_z.at[order + 2], z_sem, 3 + order, z_right))
+        elif order in (2, 4):
+            z_lefts.append(send(here, rows_z.at[order + 2], z_sem, 3 + order, z_left))
+
+    right_y, left_y, far_y = (y + 1) % 4, (y + 3) % 4, (y + 2) % 4
+    near_rows, twin_rows, rows_first, rows_onward, own_rows = [], [], [], [], []
+    mine = y * 2 + core
+
+    def send_rows(pair):
+        value = jnp.dot(
+            pick[pair],
+            rows_z[pair * 2 : pair * 2 + 2].reshape(64, 1024),
+            preferred_element_type=F32,
+        )
+        slots_out[pair] = value.astype(BF16).reshape(8, 16, 1024)
+        here = picked.at[mine, pair]
+        for way, device, rel in ((0, y_right, 0), (1, y_left, 1)):
+            expert = far_y * 2 + (core if rel == 0 else 1 - core)
+            rows_first.append(
+                send(slots_out.at[pair, expert], rows_relay.at[way, pair],
+                     rows_relay_sem, pair * 2 + way, device)
+            )
+        for way, to in ((0, right_y), (1, left_y)):
+            for rel, device in ((0, at.at_y(to)), (1, at.across_y(to))):
+                expert = to * 2 + (core if rel == 0 else 1 - core)
+                near_rows.append(
+                    send(slots_out.at[pair, expert], here, y_sem, pair * 4 + way * 2 + rel, device)
+                )
+        twin_rows.append(send(slots_out.at[pair, y * 2 + 1 - core], here, twin_sem, pair, twin))
+        own_rows.append(move(slots_out.at[pair, mine], here, 13 + pair))
+
+    def pass_rows(pair):
+        for way, device, source in (
+            (0, at.at_y(right_y), left_y), (1, at.across_y(left_y), right_y)
+        ):
+            rows_first[pair * 2 + way].wait_recv()
+            rows_onward.append(
+                send(rows_relay.at[way, pair], picked.at[source * 2 + core, pair],
+                     rows_relay_sem, 8 + pair * 2 + way, device)
+            )
+
+    def spread_rows(messages, first, count):
+        tile = one_hot(iota((128, count), 0) == first + iota((128, count), 1) % 32)
+        return jnp.dot(messages, tile, preferred_element_type=F32).astype(BF16)
+
+    next_rows(1)
+    next_rows(2)
+    arrive(by_z, [moved_z])
+    moved_y = move(message_z.at[:, y], message_y.at[:, y], 6)
+    by_y = [
+        send(message_z.at[:, (y + step) % 4], message_y.at[:, y],
+             message_sem, 7 + step, at.at_y(y + step))
+        for step in (1, 2, 3)
+    ]
+
+    passed = jnp.concatenate(
+        [message_z[block].reshape(8, 2, 128)[:, 0, :] for block in blocks], axis=0
+    ).astype(BF16)
+    slots, source = iota((512, 64), 0), iota((512, 64), 1)
+    expand = one_hot(
+        source == ((slots // 128) * 2 + (slots // 8) % 2) * 8 + (slots // 16) % 8
+    )
+    code = jnp.dot(expand, spread_rows(passed, 64, 64), preferred_element_type=F32)
+    match = (
+        (code == (slots % 2 + 1).astype(F32))
+        & (source // 32 == (slots // 8) % 2)
+        & ((source // 8) % 4 == (slots // 2) % 4)
+    )
+    pick[...] = one_hot(match).reshape(4, 128, 64)
+
+    arrive([], moved_rows)
+    send_rows(0)
+    next_rows(3)
+    send_rows(1)
+    next_rows(4)
+    next_rows(5)
+    arrive(by_y, [moved_y])
+    moved_core = move(message_y.at[:, :, core], message_all.at[tensor, :, :, core], 7)
+    by_core = send(message_y.at[:, :, 1 - core], message_all.at[tensor, :, :, core],
+                   message_sem, 0, twin)
+    send_rows(2)
+    pass_rows(0)
+    next_rows(6)
+    next_rows(7)
     arrive([by_core], [moved_core])
     here = message_all.at[tensor]
     across = send(here, here, spread_sem, 0, at.other_half())
     spread = [send(here, here, spread_sem, step, at.at_x(x + step)) for step in (1, 2, 3)]
-
-    far_copies, twin_copies = [], []
-
-    def pass_rows(order):
-        block = blocks[order]
-        arrive([y_rights[order], y_lefts[order]])
-        if order % 2 == 0:
-            here, device = rows_all.at[block, (y + 3) % 4, core], y_right
-        else:
-            here, device = rows_all.at[block, (y + 1) % 4, core], y_left
-        far_copies.append(send(here, here, far_sem, order, device))
-
-    def twin_rows(order):
-        far_copies[order].wait_recv()
-        here = rows_all.at[blocks[order], :, core]
-        twin_copies.append(send(here, here, twin_sem, order, twin))
-
-    for order in range(4):
-        pass_rows(order)
+    send_rows(3)
+    pass_rows(1)
     pass_weight(0, up_first, up_direct)
+    pass_rows(2)
     across.wait_recv()
     here = message_all.at[(1 - at.z_hi) * 4 + x]
     spread += [send(here, here, spread_sem, 3 + step, at.at_x(x + step)) for step in (1, 2, 3)]
     down_first, down_direct = send_weight(1)
-    moved_rows.wait()
-    for order in range(4, 8):
-        pass_rows(order)
-        twin_rows(order - 4)
-
-    def spread_rows(messages, first, count):
-        tile = one_hot(iota((128, count), 0) == first + iota((128, count), 1) % 32)
-        return jnp.dot(messages, tile, preferred_element_type=F32).astype(BF16)
-
-    own = message_all[tensor].reshape(64, 2, 128)[:, 0, :].astype(BF16)
-    codes = spread_rows(own, 64, 512)
-
-    @pl.loop(0, 4)
-    def _(pair):
-        slots, source = iota((128, 64), 0), iota((128, 64), 1)
-        expand = one_hot(source == (pair * 2 + (slots // 8) % 2) * 8 + slots // 16)
-        code = jnp.dot(expand, codes, preferred_element_type=F32)
-        slots, places = iota((128, 512), 0), iota((128, 512), 1)
-        match = (
-            (code == (slots % 2 + 1).astype(F32))
-            & (places // 256 == (slots // 8) % 2)
-            & ((places // 32) % 8 == slots // 16)
-            & ((places // 8) % 4 == (slots // 2) % 4)
-        )
-        pick[pair] = one_hot(match)
-
-    passed = message_z[...].reshape(64, 2, 128)[:, 0, :].astype(BF16)
+    pass_rows(3)
+
     codes, gates = spread_rows(passed, 64, 256), spread_rows(passed, 96, 256)
 
     @pl.loop(0, 8)
@@ -292,12 +380,10 @@
         for c in range(3):
             for b in range(4):
                 k, n = iota((128, 128), 0), iota((128, 128), 1)
-                here = (k - rr * 48 + b * 48 == c * 64 + n % 64) & (k >= rr * 48) & (k < rr * 48 + 48)
+                here = (k // 2 + b * 48 == c * 64 + n % 64) & (k % 2 == rr) & (k < 96)
                 order_map[b * 128 : b * 128 + 128, (rr * 3 + c) * 128 : (rr * 3 + c) * 128 + 128] = (
                     one_hot(here)
                 )
-    for order in range(4, 8):
-        twin_rows(order)
     arrive(spread)
 
     for t in range(8):
@@ -328,29 +414,20 @@
                 lanes = slice(lane * 128, lane * 128 + 128)
                 delta = jnp.zeros((48, 128), F32)
                 for r in range(16):
-                    delta = delta + right_all[r] * left_all[j * 16 + r : j * 16 + r + 1, lanes]
+                    delta = delta + right_all[r] * left_all[r * 4 + j : r * 4 + j + 1, lanes]
                 units = slice(j * 48, j * 48 + 48)
                 weight[group, half, units, lanes] = (
                     up_all[half, group, units, lanes].astype(F32) + delta
                 ).astype(BF16)
 
     pass_weight(1, down_first, down_direct)
-    for order, block in enumerate(blocks):
-        twin_copies[order].wait_recv()
-    for pair in range(4):
-        value = jnp.dot(
-            pick[pair],
-            rows_all[pair * 2 : pair * 2 + 2].reshape(512, 1024),
-            preferred_element_type=F32,
-        ).astype(BF16)
-        for group in range(8):
-            picked[pl.ds(group * 64 + pair * 16, 16), :] = value[group * 16 : group * 16 + 16]
+    arrive(near_rows + twin_rows + rows_onward, own_rows)
 
     def project(group):
         total = jnp.zeros((192, 512), F32)
         for half in (0, 1):
             total = total + lax.dot_general(
-                weight[group, half], picked[:, half * 512 : half * 512 + 512],
+                weight[group, half], picked[:, :, :, half * 512 : half * 512 + 512].reshape(512, 512),
                 (((1,), (1,)), ((), ())), preferred_element_type=F32,
             )
         part[group] = total.astype(BF16)
@@ -388,7 +465,6 @@
     arrive(down_direct[:4] + down_direct[6:], down_direct[4:6])
     arrive([far_top, far_low])
 
-    right_y, left_y, far_y = (y + 1) % 4, (y + 3) % 4, (y + 2) % 4
     twins, direct, relayed, own_slots = [], [], [], []
     for half in (0, 1):
         result[half] = (
@@ -438,7 +514,7 @@
             combine[...].reshape(512, 256), slots_in[half].reshape(512, 512)
         )
         for group in range(8):
-            line[half * 8 + group] = value[group * 32 : group * 32 + 32]
+            line[half * 8 + blocks[group]] = value[group * 32 : group * 32 + 32]
 
     rights, lefts = [], []
     for step in range(8):
@@ -474,11 +550,13 @@
             pltpu.VMEM((2, 4, 192, 512), BF16),
             pltpu.VMEM((2, 4, 192, 512), BF16),
             pltpu.VMEM((2, 2, 192, 512), BF16),
-            pltpu.VMEM((8, 4, 2, 32, 1024), BF16),
+            pltpu.VMEM((8, 32, 1024), BF16),
+            pltpu.VMEM((4, 8, 16, 1024), BF16),
+            pltpu.VMEM((2, 4, 16, 1024), BF16),
             pltpu.VMEM((8, 4, 2, 2, 128), F32),
             pltpu.VMEM((8, 4, 2, 2, 128), F32),
             pltpu.VMEM((8, 8, 4, 2, 2, 128), F32),
-            pltpu.VMEM((4, 128, 512), BF16),
+            pltpu.VMEM((4, 128, 64), BF16),
             pltpu.VMEM((8, 64, 256), BF16),
             pltpu.VMEM((512, 768), BF16),
             pltpu.VMEM((8, 64, 128), F32),
@@ -486,7 +564,7 @@
             pltpu.VMEM((16, 48, 128), F32),
             pltpu.VMEM((128, 512), F32),
             pltpu.VMEM((4, 2, 192, 512), BF16),
-            pltpu.VMEM((512, 1024), BF16),
+            pltpu.VMEM((8, 4, 16, 1024), BF16),
             pltpu.VMEM((4, 192, 512), BF16),
             pltpu.VMEM((2, 96, 512), BF16),
             pltpu.VMEM((2, 192, 512), BF16),
@@ -501,11 +579,11 @@
             pltpu.VMEM((7, 32, 512), BF16),
             pltpu.VMEM((8, 32, 512), BF16),
             pltpu.VMEM((7, 32, 512), BF16),
-            pltpu.SemaphoreType.DMA((12,)),
-            dma_sems(7),
+            pltpu.SemaphoreType.DMA((17,)),
+            dma_sems(9),
             dma_sems(16),
-            dma_sems(8),
-            dma_sems(8),
+            dma_sems(16),
+            dma_sems(4),
             dma_sems(8),
             dma_sems(8),
             dma_sems(11),
@@ -540,31 +618,17 @@
     routes,
     gates,
 ):
-    left_next, first_left_next, second_left_next = adamw_update(
-        core_left, grad_left, first_left, second_left
-    )
-    right_next, first_right_next, second_right_next = adamw_update(
-        core_right, grad_right, first_right, second_right
-    )
-    chosen = (routes[..., None] == jnp.arange(64, dtype=jnp.int32)).astype(F32)
-    taken = jnp.sum(chosen, axis=2)
-    weight = jnp.sum(chosen * gates[..., None], axis=2)
-    earlier = jnp.cumsum(taken, axis=1) - taken
-    slot = taken * (earlier + 1.0)
-    message = jnp.concatenate(
-        [
-            lax.reduce_precision(left_next, 8, 7).reshape(64, 64),
-            slot.reshape(32, 64),
-            weight.reshape(32, 64),
-            lax.reduce_precision(right_next, 8, 7).reshape(96, 64),
-            jnp.zeros((32, 64), F32),
-        ],
-        axis=0,
-    )
-    message = message.T.reshape(8, 4, 2, 2, 128)
-    x = lax.axis_index("tensor") % 4
-    rows = lax.dynamic_index_in_dim(states.reshape(32, 2, 4, 512), x, 2, keepdims=False)
-    mixed = layer(up_base[0], down_base[0], rows.reshape(32, 1024), message)
+    cores = (
+        core_left, core_right, grad_left, grad_right,
+        first_left, first_right, second_left, second_right,
+    )
+    (
+        left_next, right_next, first_left_next, first_right_next,
+        second_left_next, second_right_next, message,
+    ) = prepare(cores, routes.reshape(32, 8), gates.reshape(32, 8))
+    mixed = layer(
+        up_base[0], down_base[0], states.reshape(32, 4096), message.reshape(8, 4, 2, 2, 128)
+    )
     mixed = mixed.reshape(4, 8, 512)
     return (
         mixed,

time: 129 us -> 124 us (0.961)
  other arithmetic: 3.84 us -> 0 us
  local copies, waits for them, and re-layouts: 4.51 us -> 1.38 us
    reduce_precision x2 -> x0, other arithmetic: 2.92 us -> none  [the longest x1 1.5 us: body(): lax.reduce_precision(right_next, 8, 7).reshape(96, 64)]
    reshape x4 -> x0, local copies, waits for them, and re-layouts: 1.97 us -> none  [the longest x1 1.14 us: body(): states.reshape(32, 2, 4, 512)]
    pallas_call x0 -> x1, Pallas kernels: none -> 1.93 us  [prepare(): pl.pallas_call(prepare_kernel, out_shape=(*(jax.ShapeDtypeStruct(shape, F...]
where the time goes in v4:
time: 124 us; the launch traced here: 123 us
  Pallas kernels  121 us (98%)
  local copies, waits for them, and re-layouts  1.38 us (1%)
    pallas_call x1, Pallas kernels, layer(): pl.pallas_call(layer_kernel, out_shape=jax.ShapeDtypeStruct((32, 512), BF...  119 us

profile of v4, /device:TPU:6, one launch (start us, length us, event | category | flops | bytes accessed | tf_op | source)
XLA Modules:
  0.0 123.3 jit_solution(7962584059508120265)
XLA Ops:
  0.6 1.9 %prepare.1 = (f32[4,1024]{1,0:T(4,128)}, f32[2,3072]{1,0:T(2,128)}, f32[4,1024]{1,0:T(4,128)}, f32[2,3072]{1,0:T(2,128)}, f32[4,1024]{1,0:T(4,128)}, /*index=5*/f32[2,3072]{1,0:T(2,128)}, f32[64,2,128]{2,1,0:T(2,128)}) custom-call(f32[4,1024]{1,0:T(4,128)} %core_left.1, f32[2,3072]{1,0:T(2,128)} %core_right.1, f32[4,1024]{1,0:T(4,128)} %grad_left.1, ...), custom_call_target="tpu_custom_call" | custom-call | tf_op jit(solution)/shard_map/prepare/pallas_call | solution.py:72
  2.6 119.4 %layer.1 = bf16[32,512]{1,0:T(8,128)(2,1)} custom-call(bf16[192,4096]{1,0:T(8,128)(2,1)} %bitcast.7, bf16[192,4096]{1,0:T(8,128)(2,1)} %bitcast.8, bf16[32,4096]{1,0:T(8,128)(2,1)} %bitcast.9, f32[8,4,2,2,128]{4,3,2,1,0:T(2,128)} %bitcast.11), custom_call_target="tpu_custom_call" | custom-call | tf_op jit(solution)/shard_map/layer/pallas_call | solution.py:544
  122.0 1.4 %copy.21 = bf16[4,8,512]{2,1,0:T(8,128)(2,1)} copy(bf16[4,8,512]{2,1,0:T(8,128)(2,1)} %bitcast.10) | data formatting | bytes 65536

commit v5 on v4

--- a/solution.py
+++ b/solution.py
@@ -63,7 +63,7 @@
     row, column = (lax.broadcasted_iota(jnp.int32, (128, 128), dim) for dim in (0, 1))
     same = jnp.where(row == column, 1.0, 0.0).astype(BF16)
     for kind in range(2):
-        message[:, kind, :] = lax.dot_general(
+        message[kind] = lax.dot_general(
             entries[kind].astype(BF16), same, (((0,), (0,)), ((), ())), preferred_element_type=F32
         )
 
@@ -73,7 +73,7 @@
         prepare_kernel,
         out_shape=(
             *(jax.ShapeDtypeStruct(shape, F32) for shape in ((4, 1024), (2, 3072)) * 3),
-            jax.ShapeDtypeStruct((64, 2, 128), F32),
+            jax.ShapeDtypeStruct((2, 64, 128), F32),
         ),
         scratch_shapes=[pltpu.VMEM((2, 128, 64), F32)],
         name="prepare",
@@ -204,22 +204,24 @@
         for half, (origin, lanes) in enumerate(halves)
     ]
 
-    moved_z = move(message.at[z_lo], message_z.at[z_lo], 0)
+    moved_z = move(message.at[:, z_lo], message_z.at[:, z_lo], 0)
     by_z = [
-        send(message.at[(z_lo + step) % 8], message_z.at[z_lo], message_sem, step, same_half(step))
+        send(message.at[:, (z_lo + step) % 8], message_z.at[:, z_lo], message_sem, step, same_half(step))
         for step in range(1, 8)
     ]
 
     weights = ((up, up_all), (down, down_all))
 
-    def send_weight(w):
+    def first_weight(w):
+        return [
+            send(weights[w][0].at[:, columns_of(way, (x + 2) % 4)], relay.at[w, way],
+                 relay_sem, w * 2 + way, device)
+            for way, device in ((0, x_right), (1, x_left))
+        ]
+
+    def direct_weight(w):
         origin, dst = weights[w]
-        first, direct = [], []
-        for way, device in ((0, x_right), (1, x_left)):
-            first.append(
-                send(origin.at[:, columns_of(way, (x + 2) % 4)], relay.at[w, way],
-                     relay_sem, w * 2 + way, device)
-            )
+        direct = []
         for way, device, to in ((0, x_right, (x + 1) % 4), (1, x_left, (x + 3) % 4)):
             for half in (0, 1):
                 direct.append(
@@ -228,7 +230,7 @@
                 )
         for half in (0, 1):
             direct.append(move(origin.at[:, columns_of(half, x)], dst.at[half, x], 2 + w * 2 + half))
-        return first, direct
+        return direct
 
     def pass_weight(w, first, direct):
         dst = weights[w][1]
@@ -244,7 +246,7 @@
         for copy in own:
             copy.wait()
 
-    up_first, up_direct = send_weight(0)
+    up_first, up_direct = first_weight(0), direct_weight(0)
 
     blocks = [z_lo]
     for order in range(1, 8):
@@ -310,15 +312,15 @@
     next_rows(1)
     next_rows(2)
     arrive(by_z, [moved_z])
-    moved_y = move(message_z.at[:, y], message_y.at[:, y], 6)
+    moved_y = move(message_z.at[:, :, y], message_y.at[:, :, y], 6)
     by_y = [
-        send(message_z.at[:, (y + step) % 4], message_y.at[:, y],
+        send(message_z.at[:, :, (y + step) % 4], message_y.at[:, :, y],
              message_sem, 7 + step, at.at_y(y + step))
         for step in (1, 2, 3)
     ]
 
     passed = jnp.concatenate(
-        [message_z[block].reshape(8, 2, 128)[:, 0, :] for block in blocks], axis=0
+        [message_z[0, block].reshape(8, 128) for block in blocks], axis=0
     ).astype(BF16)
     slots, source = iota((512, 64), 0), iota((512, 64), 1)
     expand = one_hot(
@@ -332,32 +334,34 @@
     )
     pick[...] = one_hot(match).reshape(4, 128, 64)
 
+    arrive(by_y, [moved_y])
+    here = message_all.at[tensor, :, :, :, core]
+    moved_core = move(message_y.at[:, :, :, core], here, 7)
+    by_core = send(message_y.at[:, :, :, 1 - core], here, message_sem, 0, twin)
+    next_rows(3)
     arrive([], moved_rows)
     send_rows(0)
-    next_rows(3)
+    arrive([by_core], [moved_core])
+    here = message_all.at[tensor, 1]
+    across = send(here, here, spread_sem, 0, at.other_half())
+    here = message_all.at[tensor]
+    spread = [send(here, here, spread_sem, step, at.at_x(x + step)) for step in (1, 2, 3)]
+    next_rows(4)
     send_rows(1)
-    next_rows(4)
     next_rows(5)
-    arrive(by_y, [moved_y])
-    moved_core = move(message_y.at[:, :, core], message_all.at[tensor, :, :, core], 7)
-    by_core = send(message_y.at[:, :, 1 - core], message_all.at[tensor, :, :, core],
-                   message_sem, 0, twin)
+    pass_weight(0, up_first, up_direct)
+    down_first = first_weight(1)
     send_rows(2)
     pass_rows(0)
     next_rows(6)
     next_rows(7)
-    arrive([by_core], [moved_core])
-    here = message_all.at[tensor]
-    across = send(here, here, spread_sem, 0, at.other_half())
-    spread = [send(here, here, spread_sem, step, at.at_x(x + step)) for step in (1, 2, 3)]
     send_rows(3)
     pass_rows(1)
-    pass_weight(0, up_first, up_direct)
+    across.wait_recv()
+    here = message_all.at[(1 - at.z_hi) * 4 + x, 1]
+    spread += [send(here, here, spread_sem, 3 + step, at.at_x(x + step)) for step in (1, 2, 3)]
+    down_direct = direct_weight(1)
     pass_rows(2)
-    across.wait_recv()
-    here = message_all.at[(1 - at.z_hi) * 4 + x]
-    spread += [send(here, here, spread_sem, 3 + step, at.at_x(x + step)) for step in (1, 2, 3)]
-    down_first, down_direct = send_weight(1)
     pass_rows(3)
 
     codes, gates = spread_rows(passed, 64, 256), spread_rows(passed, 96, 256)
@@ -374,7 +378,11 @@
             & (places // 32 == slots // 8)
             & ((places // 8) % 4 == (slots // 2) % 4)
         )
-        combine[expert] = jnp.where(match, gate, 0.0).astype(BF16)
+        value = jnp.where(match, gate, 0.0).astype(BF16)
+        for part_at in (0, 1):
+            combine[part_at, expert] = value[
+                part_at * 32 : part_at * 32 + 32, part_at * 128 : part_at * 128 + 128
+            ]
 
     for rr in range(2):
         for c in range(3):
@@ -387,7 +395,7 @@
     arrive(spread)
 
     for t in range(8):
-        right_rows[t] = message_all[t].reshape(64, 2, 128)[:, 1, :]
+        right_rows[t] = message_all[t, 1].reshape(64, 128)
         entries[t * 16 : t * 16 + 16] = jnp.concatenate(
             [right_rows[t, pl.ds(b, 16, stride=4), :] for b in range(4)], axis=1
         ).astype(BF16)
@@ -404,137 +412,181 @@
 
     widen = jnp.where(iota((8, 512), 1) // 64 == iota((8, 512), 0), 1.0, 0.0)
 
-    @pl.loop(0, 8)
-    def _(index):
-        group, half = index // 2, index % 2
-        left = message_all[at.z_hi * 4 + group, half * 4 + x].reshape(8, 2, 128)[:, 0, :]
-        left_all[...] = contract_first(left, widen)
-        for j in range(4):
-            for lane in range(4):
-                lanes = slice(lane * 128, lane * 128 + 128)
-                delta = jnp.zeros((48, 128), F32)
-                for r in range(16):
-                    delta = delta + right_all[r] * left_all[r * 4 + j : r * 4 + j + 1, lanes]
-                units = slice(j * 48, j * 48 + 48)
-                weight[group, half, units, lanes] = (
-                    up_all[half, group, units, lanes].astype(F32) + delta
-                ).astype(BF16)
-
-    pass_weight(1, down_first, down_direct)
-    arrive(near_rows + twin_rows + rows_onward, own_rows)
-
-    def project(group):
-        total = jnp.zeros((192, 512), F32)
+    def weigh(group):
+        @pl.loop(0, 2)
+        def _(half):
+            left = message_all[at.z_hi * 4 + group, 0, half * 4 + x].reshape(8, 128)
+            left_all[...] = contract_first(left, widen)
+            for j in range(4):
+                for lane in range(4):
+                    lanes = slice(lane * 128, lane * 128 + 128)
+                    delta = jnp.zeros((48, 128), F32)
+                    for r in range(16):
+                        delta = delta + right_all[r] * left_all[r * 4 + j : r * 4 + j + 1, lanes]
+                    units = slice(j * 48, j * 48 + 48)
+                    weight[group, half, units, lanes] = (
+                        up_all[half, group, units, lanes].astype(F32) + delta
+                    ).astype(BF16)
+
+    def project(group, ab):
+        total = jnp.zeros((192, 256), F32)
         for half in (0, 1):
+            here = picked[:, ab * 2 : ab * 2 + 2, :, half * 512 : half * 512 + 512]
             total = total + lax.dot_general(
-                weight[group, half], picked[:, :, :, half * 512 : half * 512 + 512].reshape(512, 512),
+                weight[group, half], here.reshape(256, 512),
                 (((1,), (1,)), ((), ())), preferred_element_type=F32,
             )
-        part[group] = total.astype(BF16)
-
+        part[ab, group] = total.astype(BF16)
+
+    both = (0, 1)
     right_x, left_x, far_x = (x + 1) % 4, (x + 3) % 4, (x + 2) % 4
     top, low = pl.ds(0, 96), pl.ds(96, 96)
-    project(far_x)
-    copies = [
-        send(part.at[far_x, top], hidden_far.at[0], hidden_sem, 0, x_right),
-        send(part.at[far_x, low], hidden_far.at[1], hidden_sem, 1, x_left),
-    ]
-    project(right_x)
-    copies.append(send(part.at[right_x, low], hidden_near.at[0, low], hidden_sem, 2, x_right))
-    project(left_x)
-    copies.append(send(part.at[left_x, top], hidden_near.at[1, top], hidden_sem, 3, x_left))
-    copies[0].wait_recv()
-    hidden_pass[0] = (part[right_x, top].astype(F32) + hidden_far[0].astype(F32)).astype(BF16)
-    copies.append(send(hidden_pass.at[0], hidden_near.at[0, top], hidden_sem, 4, x_right))
-    copies[1].wait_recv()
-    hidden_pass[1] = (part[left_x, low].astype(F32) + hidden_far[1].astype(F32)).astype(BF16)
-    copies.append(send(hidden_pass.at[1], hidden_near.at[1, low], hidden_sem, 5, x_left))
-    project(x)
-    arrive(copies[2:])
-    value = part[x].astype(F32) + hidden_near[0].astype(F32) + hidden_near[1].astype(F32)
-    hidden[x] = (value / (1.0 + jnp.exp(-value))).astype(BF16)
-    here = hidden.at[x]
-    from_left = send(here, here, gather_sem, 0, x_right)
-    from_right = send(here, here, gather_sem, 1, x_left)
-    from_left.wait_recv()
-    here = hidden.at[left_x, top]
-    far_top = send(here, here, gather_sem, 2, x_right)
-    from_right.wait_recv()
-    here = hidden.at[right_x, low]
-    far_low = send(here, here, gather_sem, 3, x_left)
+    far_parts, near_parts = [], [[], []]
+    weigh(far_x)
+    for ab in both:
+        arrive(
+            near_rows[ab * 8 : ab * 8 + 8] + twin_rows[ab * 2 : ab * 2 + 2]
+            + rows_onward[ab * 4 : ab * 4 + 4],
+            own_rows[ab * 2 : ab * 2 + 2],
+        )
+        project(far_x, ab)
+        far_parts.append([
+            send(part.at[ab, far_x, top], hidden_far.at[ab, 0], hidden_sem, ab * 6, x_right),
+            send(part.at[ab, far_x, low], hidden_far.at[ab, 1], hidden_sem, ab * 6 + 1, x_left),
+        ])
+    weigh(right_x)
+    for ab in both:
+        project(right_x, ab)
+        near_parts[ab].append(
+            send(part.at[ab, right_x, low], hidden_near.at[ab, 0, low], hidden_sem, ab * 6 + 2, x_right)
+        )
+    weigh(left_x)
+    for ab in both:
+        project(left_x, ab)
+        near_parts[ab].append(
+            send(part.at[ab, left_x, top], hidden_near.at[ab, 1, top], hidden_sem, ab * 6 + 3, x_left)
+        )
+    for ab in both:
+        for way, device, to, units in ((0, x_right, right_x, top), (1, x_left, left_x, low)):
+            far_parts[ab][way].wait_recv()
+            hidden_pass[ab, way] = (
+                part[ab, to, units].astype(F32) + hidden_far[ab, way].astype(F32)
+            ).astype(BF16)
+            near_parts[ab].append(
+                send(hidden_pass.at[ab, way], hidden_near.at[ab, way, units],
+                     hidden_sem, ab * 6 + 4 + way, device)
+            )
+    pass_weight(1, down_first, down_direct)
+    weigh(x)
+    for ab in both:
+        project(x, ab)
+    gathers = []
+    for ab in both:
+        arrive(near_parts[ab])
+        value = (
+            part[ab, x].astype(F32)
+            + hidden_near[ab, 0].astype(F32) + hidden_near[ab, 1].astype(F32)
+        )
+        hidden[ab, x] = (value / (1.0 + jnp.exp(-value))).astype(BF16)
+        here = hidden.at[ab, x]
+        gathers.append([
+            send(here, here, gather_sem, ab * 4, x_right),
+            send(here, here, gather_sem, ab * 4 + 1, x_left),
+        ])
+    for ab in both:
+        for way, device, source, units in ((0, x_right, left_x, top), (1, x_left, right_x, low)):
+            gathers[ab][way].wait_recv()
+            here = hidden.at[ab, source, units]
+            gathers[ab].append(send(here, here, gather_sem, ab * 4 + 2 + way, device))
     arrive(down_direct[:4] + down_direct[6:], down_direct[4:6])
-    arrive([far_top, far_low])
-
-    twins, direct, relayed, own_slots = [], [], [], []
-    for half in (0, 1):
-        result[half] = (
-            contract_first(hidden[...].reshape(768, 512), down_all[half].reshape(768, 512))
-            .astype(BF16)
-            .reshape(4, 2, 64, 512)
-        )
-        twins.append(send(result.at[half, :, 1 - core], twin_in.at[half], core_sem, half, twin))
-        relayed.append(
-            send(result.at[half, far_y, core], slots_relay.at[half, 0],
-                 slots_relay_sem, half, y_right)
-        )
-        here = slots_in.at[half, y, core]
-        direct.append(send(result.at[half, right_y, core], here, slots_sem, half * 2, y_right))
-        direct.append(send(result.at[half, left_y, core], here, slots_sem, half * 2 + 1, y_left))
-        own_slots.append(move(result.at[half, y, core], here, 8 + half))
-    for half in (0, 1):
-        twins[half].wait_recv()
-        relayed.append(
-            send(twin_in.at[half, far_y], slots_relay.at[half, 1],
-                 slots_relay_sem, 2 + half, y_left)
-        )
-        here = slots_in.at[half, y, 1 - core]
-        direct.append(send(twin_in.at[half, right_y], here, slots_sem, 4 + half * 2, y_right))
-        direct.append(send(twin_in.at[half, left_y], here, slots_sem, 5 + half * 2, y_left))
-        own_slots.append(move(twin_in.at[half, y], here, 10 + half))
-    onward = []
-    for half in (0, 1):
-        relayed[half].wait_recv()
-        onward.append(
-            send(slots_relay.at[half, 0], slots_in.at[half, left_y, core],
-                 slots_relay_sem, 4 + half, y_right)
-        )
-    for half in (0, 1):
-        relayed[2 + half].wait_recv()
-        onward.append(
-            send(slots_relay.at[half, 1], slots_in.at[half, right_y, 1 - core],
-                 slots_relay_sem, 6 + half, y_left)
-        )
-    for half in (0, 1):
-        arrive(
-            [direct[half * 2], direct[half * 2 + 1], direct[4 + half * 2], direct[5 + half * 2]]
-            + [onward[half], onward[2 + half]],
-            [own_slots[half], own_slots[2 + half]],
-        )
+
+    twins, relayed, direct, onward = [], [[], []], [[], []], [[], []]
+    own_slots = [[], []]
+    for ab in both:
+        arrive(gathers[ab][2:])
+        for half in (0, 1):
+            value = contract_first(
+                hidden[ab].reshape(768, 256), down_all[half].reshape(768, 512)
+            )
+            result[ab, :, :, :, half * 512 : half * 512 + 512] = (
+                value.astype(BF16).reshape(4, 2, 32, 512)
+            )
+        twins.append(send(result.at[ab, :, 1 - core], twin_in.at[ab], core_sem, ab, twin))
+        relayed[ab].append(
+            send(result.at[ab, far_y, core], slots_relay.at[ab, 0], slots_relay_sem, ab, y_right)
+        )
+        here = slots_in.at[ab, y, core]
+        direct[ab].append(send(result.at[ab, right_y, core], here, slots_sem, ab * 2, y_right))
+        direct[ab].append(send(result.at[ab, left_y, core], here, slots_sem, ab * 2 + 1, y_left))
+        own_slots[ab].append(move(result.at[ab, y, core], here, 8 + ab))
+
+    def pass_twin(ab):
+        twins[ab].wait_recv()
+        relayed[ab].append(
+            send(twin_in.at[ab, far_y], slots_relay.at[ab, 1], slots_relay_sem, 2 + ab, y_left)
+        )
+        here = slots_in.at[ab, y, 1 - core]
+        direct[ab].append(send(twin_in.at[ab, right_y], here, slots_sem, 4 + ab * 2, y_right))
+        direct[ab].append(send(twin_in.at[ab, left_y], here, slots_sem, 5 + ab * 2, y_left))
+        own_slots[ab].append(move(twin_in.at[ab, y], here, 10 + ab))
+
+    def pass_slots(ab, way):
+        device, source, from_core = ((y_right, left_y, core), (y_left, right_y, 1 - core))[way]
+        relayed[ab][way].wait_recv()
+        onward[ab].append(
+            send(slots_relay.at[ab, way], slots_in.at[ab, source, from_core],
+                 slots_relay_sem, 4 + way * 2 + ab, device)
+        )
+
+    def mix_slots(ab):
+        arrive(direct[ab] + onward[ab], own_slots[ab])
         value = contract_first(
-            combine[...].reshape(512, 256), slots_in[half].reshape(512, 512)
-        )
-        for group in range(8):
-            line[half * 8 + blocks[group]] = value[group * 32 : group * 32 + 32]
+            combine[ab].reshape(256, 128), slots_in[ab].reshape(256, 1024)
+        )
+        for order in range(4):
+            for half in (0, 1):
+                line[half * 8 + blocks[ab * 4 + order]] = (
+                    value[order * 32 : order * 32 + 32, half * 512 : half * 512 + 512]
+                )
+
+    pass_twin(0)
+    pass_slots(0, 0)
+    pass_twin(1)
+    pass_slots(0, 1)
+    pass_slots(1, 0)
+    mix_slots(0)
+    pass_slots(1, 1)
+    mix_slots(1)
 
     rights, lefts = [], []
+    pieces = (slice(0, 16), slice(16, 32))
     for step in range(8):
-        value = line[(z + 8 - step) % 16]
-        if step > 0:
-            rights[step - 1].wait_recv()
-            value = value + right_in[step - 1].astype(F32)
-        right_out[step] = value.astype(BF16)
-        rights.append(send(right_out.at[step], right_in.at[step], right_sem, step, z_right))
-        if step < 7:
-            value = line[(z + 9 + step) % 16]
+        for piece, rows_at in enumerate(pieces):
+            value = line[(z + 8 - step) % 16, rows_at]
             if step > 0:
-                lefts[step - 1].wait_recv()
-                value = value + left_in[step - 1].astype(F32)
-            left_out[step] = value.astype(BF16)
-            lefts.append(send(left_out.at[step], left_in.at[step], left_sem, step, z_left))
-    lefts[6].wait_recv()
-    rights[7].wait_recv()
-    value = line[z] + right_in[7].astype(F32) + left_in[6].astype(F32)
-    out[...] = value.astype(BF16)
+                rights[step * 2 - 2 + piece].wait_recv()
+                value = value + right_in[step - 1, rows_at].astype(F32)
+            right_out[step, rows_at] = value.astype(BF16)
+            there = pl.ds(piece * 16, 16)
+            rights.append(
+                send(right_out.at[step, there], right_in.at[step, there],
+                     right_sem, step * 2 + piece, z_right)
+            )
+            if step < 7:
+                value = line[(z + 9 + step) % 16, rows_at]
+                if step > 0:
+                    lefts[step * 2 - 2 + piece].wait_recv()
+                    value = value + left_in[step - 1, rows_at].astype(F32)
+                left_out[step, rows_at] = value.astype(BF16)
+                lefts.append(
+                    send(left_out.at[step, there], left_in.at[step, there],
+                         left_sem, step * 2 + piece, z_left)
+                )
+    for piece, rows_at in enumerate(pieces):
+        lefts[12 + piece].wait_recv()
+        rights[14 + piece].wait_recv()
+        value = line[z, rows_at] + right_in[7, rows_at].astype(F32) + left_in[6, rows_at].astype(F32)
+        out[rows_at, :] = value.astype(BF16)
     for copy in unsent:
         copy.wait_send()
 
@@ -553,11 +605,11 @@
             pltpu.VMEM((8, 32, 1024), BF16),
             pltpu.VMEM((4, 8, 16, 1024), BF16),
             pltpu.VMEM((2, 4, 16, 1024), BF16),
-            pltpu.VMEM((8, 4, 2, 2, 128), F32),
-            pltpu.VMEM((8, 4, 2, 2, 128), F32),
-            pltpu.VMEM((8, 8, 4, 2, 2, 128), F32),
+            pltpu.VMEM((2, 8, 4, 2, 1, 128), F32),
+            pltpu.VMEM((2, 8, 4, 2, 1, 128), F32),
+            pltpu.VMEM((8, 2, 8, 4, 2, 1, 128), F32),
             pltpu.VMEM((4, 128, 64), BF16),
-            pltpu.VMEM((8, 64, 256), BF16),
+            pltpu.VMEM((2, 8, 32, 128), BF16),
             pltpu.VMEM((512, 768), BF16),
             pltpu.VMEM((8, 64, 128), F32),
             pltpu.VMEM((128, 512), BF16),
@@ -565,15 +617,15 @@
             pltpu.VMEM((128, 512), F32),
             pltpu.VMEM((4, 2, 192, 512), BF16),
             pltpu.VMEM((8, 4, 16, 1024), BF16),
-            pltpu.VMEM((4, 192, 512), BF16),
-            pltpu.VMEM((2, 96, 512), BF16),
-            pltpu.VMEM((2, 192, 512), BF16),
-            pltpu.VMEM((2, 96, 512), BF16),
-            pltpu.VMEM((4, 192, 512), BF16),
-            pltpu.VMEM((2, 4, 2, 64, 512), BF16),
-            pltpu.VMEM((2, 4, 64, 512), BF16),
-            pltpu.VMEM((2, 4, 2, 64, 512), BF16),
-            pltpu.VMEM((2, 2, 64, 512), BF16),
+            pltpu.VMEM((2, 4, 192, 256), BF16),
+            pltpu.VMEM((2, 2, 96, 256), BF16),
+            pltpu.VMEM((2, 2, 192, 256), BF16),
+            pltpu.VMEM((2, 2, 96, 256), BF16),
+            pltpu.VMEM((2, 4, 192, 256), BF16),
+            pltpu.VMEM((2, 4, 2, 32, 1024), BF16),
+            pltpu.VMEM((2, 4, 32, 1024), BF16),
+            pltpu.VMEM((2, 4, 2, 32, 1024), BF16),
+            pltpu.VMEM((2, 2, 32, 1024), BF16),
             pltpu.VMEM((16, 32, 512), F32),
             pltpu.VMEM((8, 32, 512), BF16),
             pltpu.VMEM((7, 32, 512), BF16),
@@ -588,13 +640,13 @@
             dma_sems(8),
             dma_sems(11),
             dma_sems(7),
-            dma_sems(6),
-            dma_sems(4),
+            dma_sems(12),
+            dma_sems(8),
             dma_sems(2),
             dma_sems(8),
             dma_sems(8),
-            dma_sems(8),
-            dma_sems(7),
+            dma_sems(16),
+            dma_sems(14),
         ],
         compiler_params=pltpu.CompilerParams(
             collective_id=0, has_side_effects=True, vmem_limit_bytes=VMEM_LIMIT
@@ -627,7 +679,7 @@
         second_left_next, second_right_next, message,
     ) = prepare(cores, routes.reshape(32, 8), gates.reshape(32, 8))
     mixed = layer(
-        up_base[0], down_base[0], states.reshape(32, 4096), message.reshape(8, 4, 2, 2, 128)
+        up_base[0], down_base[0], states.reshape(32, 4096), message.reshape(2, 8, 4, 2, 1, 128)
     )
     mixed = mixed.reshape(4, 8, 512)
     return (

time: 124 us -> 117 us (0.944)
  Pallas kernels: 121 us -> 114 us
    pallas_call x1, Pallas kernels: 119 us -> 112 us  [layer(): pl.pallas_call(layer_kernel, out_shape=jax.ShapeDtypeStruct((32, 512), BF...]
where the time goes in v5:
time: 117 us; the launch traced here: 116 us
  Pallas kernels  114 us (97%)
  local copies, waits for them, and re-layouts  1.38 us (1%)
    pallas_call x1, Pallas kernels, layer(): pl.pallas_call(layer_kernel, out_shape=jax.ShapeDtypeStruct((32, 512), BF...  112 us

profile of v5, /device:TPU:6, one launch (start us, length us, event | category | flops | bytes accessed | tf_op | source)
XLA Modules:
  0.0 116.0 jit_solution(12114644763688489331)
XLA Ops:
  0.6 1.9 %prepare.1 = (f32[4,1024]{1,0:T(4,128)}, f32[2,3072]{1,0:T(2,128)}, f32[4,1024]{1,0:T(4,128)}, f32[2,3072]{1,0:T(2,128)}, f32[4,1024]{1,0:T(4,128)}, /*index=5*/f32[2,3072]{1,0:T(2,128)}, f32[2,64,128]{2,1,0:T(8,128)}) custom-call(f32[4,1024]{1,0:T(4,128)} %core_left.1, f32[2,3072]{1,0:T(2,128)} %core_right.1, f32[4,1024]{1,0:T(4,128)} %grad_left.1, ...), custom_call_target="tpu_custom_call" | custom-call | tf_op jit(solution)/shard_map/prepare/pallas_call | solution.py:72
  2.6 112.1 %layer.1 = bf16[32,512]{1,0:T(8,128)(2,1)} custom-call(bf16[192,4096]{1,0:T(8,128)(2,1)} %bitcast.7, bf16[192,4096]{1,0:T(8,128)(2,1)} %bitcast.8, bf16[32,4096]{1,0:T(8,128)(2,1)} %bitcast.9, f32[2,8,4,2,1,128]{5,4,3,2,1,0:T(1,128)} %bitcast.11), custom_call_target="tpu_custom_call" | custom-call | tf_op jit(solution)/shard_map/layer/pallas_call | solution.py:596
  114.7 1.4 %copy.21 = bf16[4,8,512]{2,1,0:T(8,128)(2,1)} copy(bf16[4,8,512]{2,1,0:T(8,128)(2,1)} %bitcast.10) | data formatting | bytes 65536

commit v6 on v5

--- a/solution.py
+++ b/solution.py
@@ -148,7 +148,7 @@
 
 def layer_kernel(
     up, down, rows, message, out,
-    up_all, down_all, relay, rows_z, slots_out, rows_relay, message_z, message_y, message_all,
+    up_all, down_all, relay, rows_z, slots_out, rows_relay, message_z, message_y, message_own, left_in_x,
     pick, combine, order_map, right_rows, entries, right_all, left_all, weight, picked,
     part, hidden_far, hidden_near, hidden_pass, hidden,
     result, twin_in, slots_in, slots_relay, line, right_in, left_in, right_out, left_out,
@@ -204,9 +204,11 @@
         for half, (origin, lanes) in enumerate(halves)
     ]
 
-    moved_z = move(message.at[:, z_lo], message_z.at[:, z_lo], 0)
+    here = message_z.at[:, z_lo // 4, z_lo % 4]
+    moved_z = move(message.at[:, z_lo // 4, z_lo % 4], here, 0)
     by_z = [
-        send(message.at[:, (z_lo + step) % 8], message_z.at[:, z_lo], message_sem, step, same_half(step))
+        send(message.at[:, ((z_lo + step) % 8) // 4, (z_lo + step) % 4], here,
+             message_sem, step, same_half(step))
         for step in range(1, 8)
     ]
 
@@ -312,15 +314,15 @@
     next_rows(1)
     next_rows(2)
     arrive(by_z, [moved_z])
-    moved_y = move(message_z.at[:, :, y], message_y.at[:, :, y], 6)
+    moved_y = move(message_z.at[:, :, :, y], message_y.at[:, :, :, y], 6)
     by_y = [
-        send(message_z.at[:, :, (y + step) % 4], message_y.at[:, :, y],
+        send(message_z.at[:, :, :, (y + step) % 4], message_y.at[:, :, :, y],
              message_sem, 7 + step, at.at_y(y + step))
         for step in (1, 2, 3)
     ]
 
     passed = jnp.concatenate(
-        [message_z[0, block].reshape(8, 128) for block in blocks], axis=0
+        [message_z[0, block // 4, block % 4].reshape(8, 128) for block in blocks], axis=0
     ).astype(BF16)
     slots, source = iota((512, 64), 0), iota((512, 64), 1)
     expand = one_hot(
@@ -335,17 +337,26 @@
     pick[...] = one_hot(match).reshape(4, 128, 64)
 
     arrive(by_y, [moved_y])
-    here = message_all.at[tensor, :, :, :, core]
-    moved_core = move(message_y.at[:, :, :, core], here, 7)
-    by_core = send(message_y.at[:, :, :, 1 - core], here, message_sem, 0, twin)
+    here = message_own.at[:, :, :, :, core]
+    moved_core = move(message_y.at[:, :, :, :, core], here, 7)
+    by_core = send(message_y.at[:, :, :, :, 1 - core], here, message_sem, 0, twin)
     next_rows(3)
     arrive([], moved_rows)
     send_rows(0)
     arrive([by_core], [moved_core])
-    here = message_all.at[tensor, 1]
+    right_rows[...] = message_own[1].reshape(64, 128)
+    entries[tensor] = jnp.concatenate(
+        [right_rows[pl.ds(b, 16, stride=4), :] for b in range(4)], axis=1
+    ).astype(BF16)
+    here = entries.at[tensor]
     across = send(here, here, spread_sem, 0, at.other_half())
-    here = message_all.at[tensor]
     spread = [send(here, here, spread_sem, step, at.at_x(x + step)) for step in (1, 2, 3)]
+    moved_left = move(message_own.at[0, :, x], left_in_x.at[x], 17)
+    spread += [
+        send(message_own.at[0, :, (x + step) % 4], left_in_x.at[x],
+             spread_sem, 6 + step, at.at_x(x + step))
+        for step in (1, 2, 3)
+    ]
     next_rows(4)
     send_rows(1)
     next_rows(5)
@@ -358,7 +369,7 @@
     send_rows(3)
     pass_rows(1)
     across.wait_recv()
-    here = message_all.at[(1 - at.z_hi) * 4 + x, 1]
+    here = entries.at[(1 - at.z_hi) * 4 + x]
     spread += [send(here, here, spread_sem, 3 + step, at.at_x(x + step)) for step in (1, 2, 3)]
     down_direct = direct_weight(1)
     pass_rows(2)
@@ -392,14 +403,11 @@
                 order_map[b * 128 : b * 128 + 128, (rr * 3 + c) * 128 : (rr * 3 + c) * 128 + 128] = (
                     one_hot(here)
                 )
-    arrive(spread)
-
-    for t in range(8):
-        right_rows[t] = message_all[t, 1].reshape(64, 128)
-        entries[t * 16 : t * 16 + 16] = jnp.concatenate(
-            [right_rows[t, pl.ds(b, 16, stride=4), :] for b in range(4)], axis=1
-        ).astype(BF16)
-    placed = jnp.dot(entries[...], order_map[...], preferred_element_type=F32)
+    arrive(spread, [moved_left])
+
+    placed = jnp.dot(
+        entries[...].reshape(128, 512), order_map[...], preferred_element_type=F32
+    )
     for t in range(8):
         for rr in range(2):
             for c in range(3):
@@ -415,7 +423,7 @@
     def weigh(group):
         @pl.loop(0, 2)
         def _(half):
-            left = message_all[at.z_hi * 4 + group, 0, half * 4 + x].reshape(8, 128)
+            left = left_in_x[group, half].reshape(8, 128)
             left_all[...] = contract_first(left, widen)
             for j in range(4):
                 for lane in range(4):
@@ -605,14 +613,15 @@
             pltpu.VMEM((8, 32, 1024), BF16),
             pltpu.VMEM((4, 8, 16, 1024), BF16),
             pltpu.VMEM((2, 4, 16, 1024), BF16),
-            pltpu.VMEM((2, 8, 4, 2, 1, 128), F32),
-            pltpu.VMEM((2, 8, 4, 2, 1, 128), F32),
-            pltpu.VMEM((8, 2, 8, 4, 2, 1, 128), F32),
+            pltpu.VMEM((2, 2, 4, 4, 2, 1, 128), F32),
+            pltpu.VMEM((2, 2, 4, 4, 2, 1, 128), F32),
+            pltpu.VMEM((2, 2, 4, 4, 2, 1, 128), F32),
+            pltpu.VMEM((4, 2, 4, 2, 1, 128), F32),
             pltpu.VMEM((4, 128, 64), BF16),
             pltpu.VMEM((2, 8, 32, 128), BF16),
             pltpu.VMEM((512, 768), BF16),
-            pltpu.VMEM((8, 64, 128), F32),
-            pltpu.VMEM((128, 512), BF16),
+            pltpu.VMEM((64, 128), F32),
+            pltpu.VMEM((8, 16, 512), BF16),
             pltpu.VMEM((16, 48, 128), F32),
             pltpu.VMEM((128, 512), F32),
             pltpu.VMEM((4, 2, 192, 512), BF16),
@@ -631,7 +640,7 @@
             pltpu.VMEM((7, 32, 512), BF16),
             pltpu.VMEM((8, 32, 512), BF16),
             pltpu.VMEM((7, 32, 512), BF16),
-            pltpu.SemaphoreType.DMA((17,)),
+            pltpu.SemaphoreType.DMA((18,)),
             dma_sems(9),
             dma_sems(16),
             dma_sems(16),
@@ -639,7 +648,7 @@
             dma_sems(8),
             dma_sems(8),
             dma_sems(11),
-            dma_sems(7),
+            dma_sems(10),
             dma_sems(12),
             dma_sems(8),
             dma_sems(2),
@@ -679,7 +688,7 @@
         second_left_next, second_right_next, message,
     ) = prepare(cores, routes.reshape(32, 8), gates.reshape(32, 8))
     mixed = layer(
-        up_base[0], down_base[0], states.reshape(32, 4096), message.reshape(2, 8, 4, 2, 1, 128)
+        up_base[0], down_base[0], states.reshape(32, 4096), message.reshape(2, 2, 4, 4, 2, 1, 128)
     )
     mixed = mixed.reshape(4, 8, 512)
     return (

time: 117 us -> 115 us (0.983)
  Pallas kernels: 114 us -> 112 us
    pallas_call x1, Pallas kernels: 112 us -> 110 us  [layer(): pl.pallas_call(layer_kernel, out_shape=jax.ShapeDtypeStruct((32, 512), BF...]
where the time goes in v6:
time: 115 us; the launch traced here: 114 us
  Pallas kernels  112 us (97%)
  local copies, waits for them, and re-layouts  1.38 us (1%)
    pallas_call x1, Pallas kernels, layer(): pl.pallas_call(layer_kernel, out_shape=jax.ShapeDtypeStruct((32, 512), BF...  110 us

profile of v6, /device:TPU:6, one launch (start us, length us, event | category | flops | bytes accessed | tf_op | source)
XLA Modules:
  0.0 113.8 jit_solution(17076010485230696531)
XLA Ops:
  0.6 1.9 %prepare.1 = (f32[4,1024]{1,0:T(4,128)}, f32[2,3072]{1,0:T(2,128)}, f32[4,1024]{1,0:T(4,128)}, f32[2,3072]{1,0:T(2,128)}, f32[4,1024]{1,0:T(4,128)}, /*index=5*/f32[2,3072]{1,0:T(2,128)}, f32[2,64,128]{2,1,0:T(8,128)}) custom-call(f32[4,1024]{1,0:T(4,128)} %core_left.1, f32[2,3072]{1,0:T(2,128)} %core_right.1, f32[4,1024]{1,0:T(4,128)} %grad_left.1, ...), custom_call_target="tpu_custom_call" | custom-call | tf_op jit(solution)/shard_map/prepare/pallas_call | solution.py:72
  2.6 109.9 %layer.1 = bf16[32,512]{1,0:T(8,128)(2,1)} custom-call(bf16[192,4096]{1,0:T(8,128)(2,1)} %bitcast.7, bf16[192,4096]{1,0:T(8,128)(2,1)} %bitcast.8, bf16[32,4096]{1,0:T(8,128)(2,1)} %bitcast.9, f32[2,2,4,4,2,1,128]{6,5,4,3,2,1,0:T(1,128)} %bitcast.11), custom_call_target="tpu_custom_call" | custom-call | tf_op jit(solution)/shard_map/layer/pallas_call | solution.py:604
  112.4 1.4 %copy.21 = bf16[4,8,512]{2,1,0:T(8,128)(2,1)} copy(bf16[4,8,512]{2,1,0:T(8,128)(2,1)} %bitcast.10) | data formatting | bytes 65536

commit v7 on v6

--- a/solution.py
+++ b/solution.py
@@ -310,6 +310,15 @@
     def spread_rows(messages, first, count):
         tile = one_hot(iota((128, count), 0) == first + iota((128, count), 1) % 32)
         return jnp.dot(messages, tile, preferred_element_type=F32).astype(BF16)
+
+    for rr in range(2):
+        for c in range(3):
+            for b in range(4):
+                k, n = iota((128, 128), 0), iota((128, 128), 1)
+                here = (k // 2 + b * 48 == c * 64 + n % 64) & (k % 2 == rr) & (k < 96)
+                order_map[b * 128 : b * 128 + 128, (rr * 3 + c) * 128 : (rr * 3 + c) * 128 + 128] = (
+                    one_hot(here)
+                )
 
     next_rows(1)
     next_rows(2)
@@ -375,34 +384,6 @@
     pass_rows(2)
     pass_rows(3)
 
-    codes, gates = spread_rows(passed, 64, 256), spread_rows(passed, 96, 256)
-
-    @pl.loop(0, 8)
-    def _(expert):
-        slots, source = iota((64, 64), 0), iota((64, 64), 1)
-        expand = one_hot(source == (slots // 8) * 8 + expert)
-        code = jnp.dot(expand, codes, preferred_element_type=F32)
-        gate = jnp.dot(expand, gates, preferred_element_type=F32)
-        slots, places = iota((64, 256), 0), iota((64, 256), 1)
-        match = (
-            (code == (slots % 2 + 1).astype(F32))
-            & (places // 32 == slots // 8)
-            & ((places // 8) % 4 == (slots // 2) % 4)
-        )
-        value = jnp.where(match, gate, 0.0).astype(BF16)
-        for part_at in (0, 1):
-            combine[part_at, expert] = value[
-                part_at * 32 : part_at * 32 + 32, part_at * 128 : part_at * 128 + 128
-            ]
-
-    for rr in range(2):
-        for c in range(3):
-            for b in range(4):
-                k, n = iota((128, 128), 0), iota((128, 128), 1)
-                here = (k // 2 + b * 48 == c * 64 + n % 64) & (k % 2 == rr) & (k < 96)
-                order_map[b * 128 : b * 128 + 128, (rr * 3 + c) * 128 : (rr * 3 + c) * 128 + 128] = (
-                    one_hot(here)
-                )
     arrive(spread, [moved_left])
 
     placed = jnp.dot(
@@ -506,15 +487,50 @@
             gathers[ab][way].wait_recv()
             here = hidden.at[ab, source, units]
             gathers[ab].append(send(here, here, gather_sem, ab * 4 + 2 + way, device))
+
+    codes, gates = spread_rows(passed, 64, 256), spread_rows(passed, 96, 256)
+
+    @pl.loop(0, 8)
+    def _(expert):
+        slots, source = iota((64, 64), 0), iota((64, 64), 1)
+        expand = one_hot(source == (slots // 8) * 8 + expert)
+        code = jnp.dot(expand, codes, preferred_element_type=F32)
+        gate = jnp.dot(expand, gates, preferred_element_type=F32)
+        slots, places = iota((64, 256), 0), iota((64, 256), 1)
+        match = (
+            (code == (slots % 2 + 1).astype(F32))
+            & (places // 32 == slots // 8)
+            & ((places // 8) % 4 == (slots // 2) % 4)
+        )
+        value = jnp.where(match, gate, 0.0).astype(BF16)
+        for part_at in (0, 1):
+            combine[part_at, expert] = value[
+                part_at * 32 : part_at * 32 + 32, part_at * 128 : part_at * 128 + 128
+            ]
+
     arrive(down_direct[:4] + down_direct[6:], down_direct[4:6])
 
     twins, relayed, direct, onward = [], [[], []], [[], []], [[], []]
     own_slots = [[], []]
+
+    def pass_twin(ab):
+        twins[ab].wait_recv()
+        relayed[ab].append(
+            send(twin_in.at[ab, far_y], slots_relay.at[ab, 1], slots_relay_sem, 2 + ab, y_left)
+        )
+        here = slots_in.at[ab, y, 1 - core]
+        direct[ab].append(send(twin_in.at[ab, right_y], here, slots_sem, 4 + ab * 2, y_right))
+        direct[ab].append(send(twin_in.at[ab, left_y], here, slots_sem, 5 + ab * 2, y_left))
+        own_slots[ab].append(move(twin_in.at[ab, y], here, 10 + ab))
+
     for ab in both:
         arrive(gathers[ab][2:])
+        if ab == 1:
+            pass_twin(0)
+        turned = hidden[ab].reshape(768, 256).T
         for half in (0, 1):
-            value = contract_first(
-                hidden[ab].reshape(768, 256), down_all[half].reshape(768, 512)
+            value = jnp.dot(
+                turned, down_all[half].reshape(768, 512), preferred_element_type=F32
             )
             result[ab, :, :, :, half * 512 : half * 512 + 512] = (
                 value.astype(BF16).reshape(4, 2, 32, 512)
@@ -528,16 +544,6 @@
         direct[ab].append(send(result.at[ab, left_y, core], here, slots_sem, ab * 2 + 1, y_left))
         own_slots[ab].append(move(result.at[ab, y, core], here, 8 + ab))
 
-    def pass_twin(ab):
-        twins[ab].wait_recv()
-        relayed[ab].append(
-            send(twin_in.at[ab, far_y], slots_relay.at[ab, 1], slots_relay_sem, 2 + ab, y_left)
-        )
-        here = slots_in.at[ab, y, 1 - core]
-        direct[ab].append(send(twin_in.at[ab, right_y], here, slots_sem, 4 + ab * 2, y_right))
-        direct[ab].append(send(twin_in.at[ab, left_y], here, slots_sem, 5 + ab * 2, y_left))
-        own_slots[ab].append(move(twin_in.at[ab, y], here, 10 + ab))
-
     def pass_slots(ab, way):
         device, source, from_core = ((y_right, left_y, core), (y_left, right_y, 1 - core))[way]
         relayed[ab][way].wait_recv()
@@ -557,7 +563,6 @@
                     value[order * 32 : order * 32 + 32, half * 512 : half * 512 + 512]
                 )
 
-    pass_twin(0)
     pass_slots(0, 0)
     pass_twin(1)
     pass_slots(0, 1)

time: 115 us -> 115 us (level)
  no operation moved by 1% of the time
where the time goes in v7:
time: 115 us; the launch traced here: 114 us
  Pallas kernels  112 us (97%)
  local copies, waits for them, and re-layouts  1.38 us (1%)
    pallas_call x1, Pallas kernels, layer(): pl.pallas_call(layer_kernel, out_shape=jax.ShapeDtypeStruct((32, 512), BF...  111 us

profile of v7, /device:TPU:6, one launch (start us, length us, event | category | flops | bytes accessed | tf_op | source)
XLA Modules:
  0.0 114.5 jit_solution(14847262517992172631)
XLA Ops:
  0.6 1.9 %prepare.1 = (f32[4,1024]{1,0:T(4,128)}, f32[2,3072]{1,0:T(2,128)}, f32[4,1024]{1,0:T(4,128)}, f32[2,3072]{1,0:T(2,128)}, f32[4,1024]{1,0:T(4,128)}, /*index=5*/f32[2,3072]{1,0:T(2,128)}, f32[2,64,128]{2,1,0:T(8,128)}) custom-call(f32[4,1024]{1,0:T(4,128)} %core_left.1, f32[2,3072]{1,0:T(2,128)} %core_right.1, f32[4,1024]{1,0:T(4,128)} %grad_left.1, ...), custom_call_target="tpu_custom_call" | custom-call | tf_op jit(solution)/shard_map/prepare/pallas_call | solution.py:72
  2.6 110.5 %layer.1 = bf16[32,512]{1,0:T(8,128)(2,1)} custom-call(bf16[192,4096]{1,0:T(8,128)(2,1)} %bitcast.7, bf16[192,4096]{1,0:T(8,128)(2,1)} %bitcast.8, bf16[32,4096]{1,0:T(8,128)(2,1)} %bitcast.9, f32[2,2,4,4,2,1,128]{6,5,4,3,2,1,0:T(1,128)} %bitcast.11), custom_call_target="tpu_custom_call" | custom-call | tf_op jit(solution)/shard_map/layer/pallas_call | solution.py:609
  113.1 1.4 %copy.21 = bf16[4,8,512]{2,1,0:T(8,128)(2,1)} copy(bf16[4,8,512]{2,1,0:T(8,128)(2,1)} %bitcast.10) | data formatting | bytes 65536
